TPU v7x, 256 devices: a whole 4x4x8 slice. The times are simulated.
256 devices in a mesh: doc: 4 (over y), span: 8 (over z_lo, core), tp: 8 (over x, z_hi).
Axes of the slice: x: 4, y: 4, z: 8 (z_hi: 2, z_lo: 4; z = z_hi * 4 + z_lo), core: 2. Of those that a mesh axis runs over, the one named last changes fastest.
Arguments:
- encoded: bfloat16 [32768, 1024], P(('doc', 'span', 'tp')), may hold values from -12 to 12
- span_lens: int32 [512], P(('doc', 'span')), may hold values from 1 to 64, as said below
- kv_weight: bfloat16 [1024, 8, 256], P(None, 'tp'), may hold values from -0.1875 to 0.1875
- queries: bfloat16 [1024, 8, 1024], P(('doc', 'span'), 'tp'), may hold values from -80 to 80
- out_weight: bfloat16 [8, 1024, 8192], P('tp', None, ('doc', 'span')), may hold values from -0.375 to 0.375
- residual: bfloat16 [1024, 8192], P('tp', ('doc', 'span')), may hold values from -6 to 6
Outputs:
- mixed: bfloat16 [1024, 8192], P('tp', ('doc', 'span'))
Inputs may be any that keep to these rules, and one draw needn't show every extreme that they name: `span_lens`: the first span has all 64 rows valid.
All inputs are finite; a program needn't handle non-finite values.
Results may differ from a plain program's by a relative error of at most 0.019.
The roundings to bfloat16 on the way count: a program that leaves them out, or rounds other values in their place, can miss the bound.
Values may be sent and summed in bfloat16 or wider, within the bound.
No kernel may reach another device: no remote copies, remote signals or barrier semaphores. Data moves between devices by JAX's collectives and lax.ppermute only.
A program may use at most 64 MiB of HBM per device.

v0:
```python
import functools

import jax
import jax.numpy as jnp
from jax import lax
from jax.experimental import pallas as pl
from jax.experimental.pallas import tpu as pltpu
from jax.sharding import PartitionSpec as P

SPAN = 64
HD = 128
GROUP = 8
AXES = ("doc", "span", "tp")
Z_ORDER = (0, 2, 1, 3)
EXP2_SCALE = HD**-0.5 * 1.4426950408889634
f32, bf16 = jnp.float32, jnp.bfloat16


def move(value, target):
    def index(y, z, c, x, h):
        return ((y % 4 * 4 + z % 4) * 2 + c % 2) * 8 + x % 4 * 2 + h % 2

    pairs = [
        (index(y, z, c, x, h), index(*target(y, z, c, x, h)))
        for y in range(4)
        for z in range(4)
        for c in range(2)
        for x in range(4)
        for h in range(2)
    ]
    return lax.ppermute(value, AXES, pairs)


def from_x(value, k):
    return move(value, lambda y, z, c, x, h: (y, z, c, x - k, h))


def from_y(value, k):
    return move(value, lambda y, z, c, x, h: (y - k, z, c, x, h))


def swap_z(value, step):
    return move(value, lambda y, z, c, x, h: (y, z ^ step, c, x, h))


def other_core(value):
    return move(value, lambda y, z, c, x, h: (y, z, c + 1, x, h))


def other_half(value):
    return move(value, lambda y, z, c, x, h: (y, z, c, x, h + 1))


def vmem(count):
    return [pl.BlockSpec(memory_space=pltpu.VMEM)] * count


ANY = pl.BlockSpec(memory_space=pl.ANY)
SMEM = pl.BlockSpec(memory_space=pltpu.SMEM)
PARAMS = pltpu.CompilerParams(vmem_limit_bytes=40 * 1024 * 1024)


def cost(flops, nbytes, exps=0):
    return pl.CostEstimate(flops=flops, bytes_accessed=nbytes, transcendentals=exps)


def span_pair(place_ref, lens_ref, k, flip):
    x = place_ref[1]
    h = place_ref[2]
    half = (1 - h) if flip else h
    return (lax.rem(x + k, 4) * 2 + half) * 2


def project_kernel(flip, place_ref, lens_ref, e0, e1, e2, e3, weight, *rest):
    out = rest[-1]
    rows = lax.broadcasted_iota(jnp.int32, (SPAN, HD), 0)
    lane = lax.broadcasted_iota(jnp.int32, (16, 2 * HD), 1)
    lens = jnp.zeros((16, 2 * HD), f32)
    for k, block in enumerate((e0, e1, e2, e3)):
        both = jnp.dot(block[...], weight[...], preferred_element_type=f32)
        first = span_pair(place_ref, lens_ref, k, flip)
        for s in range(2):
            part = both[s * SPAN : (s + 1) * SPAN]
            valid = rows < lens_ref[first + s]
            keys = part[:, :HD]
            keys = jnp.where(valid, keys, keys[:1])
            values = jnp.where(valid, part[:, HD:], 0.0)
            at = k * 2 * SPAN + s * SPAN
            out[at : at + SPAN, :HD] = keys.astype(bf16)
            out[at : at + SPAN, HD:] = values.astype(bf16)
            lens = jnp.where(lane == 2 * k + s, lens_ref[first + s].astype(f32), lens)
    out[512:] = lens.astype(bf16)


def project(flip, place, lens, blocks, weight, after=()):
    return pl.pallas_call(
        functools.partial(project_kernel, flip),
        out_shape=jax.ShapeDtypeStruct((528, 2 * HD), bf16),
        in_specs=[SMEM, SMEM] + vmem(5) + [ANY] * len(after),
        out_specs=vmem(1)[0],
        compiler_params=PARAMS,
        cost_estimate=cost(2 * 512 * 1024 * 256, 2 << 20),
        name="project",
    )(place, lens, *blocks, weight, *after)


def split3(value):
    high = value.astype(bf16)
    rest = value - high.astype(f32)
    middle = rest.astype(bf16)
    low = (rest - middle.astype(f32)).astype(bf16)
    return high, middle, low


def put_stats(out, at, stats):
    for i, term in enumerate(split3(stats)):
        out[at : at + 2 * GROUP, i * HD : (i + 1) * HD] = term
    out[at : at + 2 * GROUP, 3 * HD :] = jnp.zeros((2 * GROUP, (GROUP - 3) * HD), bf16)


def get_stats(part, at):
    terms = [part[at : at + 2 * GROUP, i * HD : (i + 1) * HD].astype(f32) for i in range(3)]
    return (terms[0] + terms[1]) + terms[2]


def attend_kernel(queries, parts, carries, valued, emit):
    rows = lax.broadcasted_iota(jnp.int32, (SPAN, HD), 0).astype(f32)
    for p, part in enumerate(parts):
        valued[p * 512 : (p + 1) * 512, :HD] = part[:512, HD:]
        lens = part[512:, :HD].astype(f32)
        for i in range(8):
            at = p * 512 + i * SPAN
            valid = rows < lens[:1, i : i + 1]
            valued[at : at + SPAN, HD:] = jnp.where(valid, 1.0, 0.0).astype(bf16)
    count = queries[0].shape[0]
    lane = lax.broadcasted_iota(jnp.int32, (count, HD), 1)
    step = 4
    tiles = [(i, g) for i in range(len(queries)) for g in range(0, GROUP, step)]

    def scores_of(i, g):
        q = jnp.concatenate(
            [queries[i][:, h * HD : (h + 1) * HD] for h in range(g, g + step)], axis=0
        )
        return [
            lax.dot_general(
                q, part[:512, :HD], (((1,), (1,)), ((), ())), preferred_element_type=f32
            )
            for part in parts
        ]

    ahead = scores_of(*tiles[0])
    for n, (i, g) in enumerate(tiles):
        scores = ahead
        if n + 1 < len(tiles):
            ahead = scores_of(*tiles[n + 1])
        if g == 0:
            packed = jnp.zeros((count, HD), f32)
            sums = [None] * GROUP
        top = functools.reduce(
            jnp.maximum,
            [block[:, a : a + HD] for block in scores for a in range(0, 512, HD)],
        )
        top = jnp.max(top, axis=-1, keepdims=True)
        if carries[i] is not None:
            before, before_stats = carries[i]
            old = jnp.concatenate([before_stats[:, h : h + 1] for h in range(g, g + step)], axis=0)
            top = jnp.maximum(top, old)
            shrink = jnp.exp2((old - top) * EXP2_SCALE)
        total = jnp.zeros((step * count, 2 * HD), f32)
        for p, block in enumerate(scores):
            probs = jnp.exp2((block - top) * EXP2_SCALE).astype(bf16)
            total += jnp.dot(
                probs, valued[p * 512 : (p + 1) * 512], preferred_element_type=f32
            )
        for j in range(step):
            h = g + j
            here = slice(j * count, (j + 1) * count)
            summed, weight = total[here, :HD], total[here, HD:]
            if carries[i] is not None:
                summed += before[:, h * HD : (h + 1) * HD] * shrink[here]
                weight += before_stats[:, GROUP + h : GROUP + h + 1] * shrink[here]
            sums[h] = summed
            packed = jnp.where(lane == h, top[here], packed)
            packed = jnp.where(lane == GROUP + h, weight, packed)
        if g + step == GROUP:
            emit(i, sums, packed)


def near_kernel(q0, q1, q2, q3, n0, n1, n2, n3, q_all, sums_all, stats_all, valued):
    queries = (q0, q1, q2, q3)
    for i, q in enumerate(queries):
        q_all[i] = q[...]

    def emit(i, sums, packed):
        for h, value in enumerate(sums):
            sums_all[i, :, h * HD : (h + 1) * HD] = value
        stats_all[i] = packed

    attend_kernel(queries, (n0, n1, n2, n3), (None,) * 4, valued, emit)


def attend_near(queries, kv):
    count = queries[0].shape[0]
    return pl.pallas_call(
        near_kernel,
        out_shape=(
            jax.ShapeDtypeStruct((4, count, GROUP * HD), bf16),
            jax.ShapeDtypeStruct((4, count, GROUP * HD), f32),
            jax.ShapeDtypeStruct((4, count, HD), f32),
        ),
        in_specs=vmem(8),
        out_specs=tuple(vmem(3)),
        scratch_shapes=[pltpu.VMEM((2048, 2 * HD), bf16)],
        compiler_params=PARAMS,
        cost_estimate=cost(4 * 2048 * 2048 * 256, 3 << 20, 2048 * 2048),
        name="attend_near",
    )(*queries, *kv)


def far_kernel(k, place_ref, q_all, n0, n1, n2, n3, sums_all, stats_all, out, valued):
    count = q_all.shape[1]
    at = lax.rem(place_ref[1] + k, 4)

    def emit(i, sums, packed):
        for h, value in enumerate(sums):
            out[:count, h * HD : (h + 1) * HD] = value.astype(bf16)
        packed = jnp.concatenate([packed, jnp.zeros((HD - count, HD), f32)], axis=0)
        put_stats(out, count, packed.T[: 2 * GROUP])

    carry = (sums_all.at[at], stats_all[at])
    attend_kernel((q_all.at[at],), (n0, n1, n2, n3), (carry,), valued, emit)


def attend_far(k, place, carries, kv):
    q_all, sums_all, stats_all = carries
    count = q_all.shape[1]
    return pl.pallas_call(
        functools.partial(far_kernel, k),
        out_shape=jax.ShapeDtypeStruct((count + 2 * GROUP, GROUP * HD), bf16),
        in_specs=[SMEM] + vmem(7),
        out_specs=vmem(1)[0],
        scratch_shapes=[pltpu.VMEM((2048, 2 * HD), bf16)],
        compiler_params=PARAMS,
        cost_estimate=cost(4 * 512 * 2048 * 256, 2 << 20, 512 * 2048),
        name="attend_far",
    )(place, q_all, *kv, sums_all, stats_all)


def by_rows(array):
    return jnp.concatenate([array, jnp.zeros((HD - array.shape[0], HD), f32)], axis=0).T


def fold_kernel(count, last, *refs):
    parts, out = refs[:-1], refs[-1]
    stats = [get_stats(part, count) for part in parts]
    half = count // 2
    if last:
        lane = lax.broadcasted_iota(jnp.int32, stats[1].shape, 1)
        ahead, back = (pltpu.roll(stats[1], r, axis=1) for r in (HD - half, half))
        stats[1] = jnp.where(lane < half, ahead, back)
    tops = [s[:GROUP] for s in stats]
    top = functools.reduce(jnp.maximum, tops)
    factors = [jnp.exp2((t - top) * EXP2_SCALE) for t in tops]
    total = sum(f * s[GROUP:] for f, s in zip(factors, stats))
    if last:
        factors = [f / total for f in factors]
    else:
        put_stats(out, count, jnp.concatenate([top, total], axis=0))
    factors = [by_rows(f)[:count] for f in factors]
    for g in range(GROUP):
        lanes = slice(g * HD, (g + 1) * HD)
        pieces = [part[:count, lanes].astype(f32) for part in parts]
        if last:
            pieces[1] = jnp.concatenate([pieces[1][half:], pieces[1][:half]], axis=0)
        out[:count, lanes] = sum(
            piece * f[:, g : g + 1] for piece, f in zip(pieces, factors)
        ).astype(bf16)


def fold(count, parts, last=False):
    return pl.pallas_call(
        functools.partial(fold_kernel, count, last),
        out_shape=jax.ShapeDtypeStruct((count + (0 if last else 2 * GROUP), GROUP * HD), bf16),
        in_specs=vmem(len(parts)),
        out_specs=vmem(1)[0],
        compiler_params=PARAMS,
        cost_estimate=cost(8 * count * 1024, len(parts) * count << 11),
        name="fold",
    )(*parts)


def output_kernel(place_ref, own, beside, other, weights, o0, o1, o2, o3, rows):
    y, z, c = place_ref[0], place_ref[3], place_ref[4]
    blocks = [own.at[:32], own.at[32:], beside.at[:32], beside.at[32:]]
    blocks += [other.at[i * 32 : (i + 1) * 32] for i in range(4)]
    for i, block in enumerate(blocks):
        core = (1 - c) if i >= 4 else c
        at = (jnp.bitwise_xor(z, Z_ORDER[i % 4]) * 2 + core) * 32
        rows[pl.ds(pl.multiple_of(at, 32), 32), :] = block[...]
    for j, out in enumerate((o0, o1, o2, o3)):
        weight = weights[lax.rem(y + j, 4)]
        out[...] = jnp.dot(rows[...], weight, preferred_element_type=f32).astype(bf16)


def output_terms(place, own, beside, other, weights):
    return pl.pallas_call(
        output_kernel,
        out_shape=tuple([jax.ShapeDtypeStruct((256, 256), bf16)] * 4),
        in_specs=[SMEM] + vmem(4),
        out_specs=tuple(vmem(4)),
        scratch_shapes=[pltpu.VMEM((256, GROUP * HD), bf16)],
        compiler_params=PARAMS,
        cost_estimate=cost(2 * 256 * 1024 * 1024, 3 << 20),
        name="output",
    )(place, own, beside, other, weights)


def sum_kernel(place_ref, t0, t1, t2, t3, mine, other):
    h = place_ref[2]
    for out, half in ((mine, h), (other, 1 - h)):
        at = pl.ds(pl.multiple_of(half * 128, 128), 128)
        out[...] = sum(t[at, :].astype(f32) for t in (t0, t1, t2, t3)).astype(out.dtype)


def sum_terms(place, terms):
    return pl.pallas_call(
        sum_kernel,
        out_shape=(
            jax.ShapeDtypeStruct((128, 256), f32),
            jax.ShapeDtypeStruct((128, 256), bf16),
        ),
        in_specs=[SMEM] + vmem(4),
        out_specs=tuple(vmem(2)),
        compiler_params=PARAMS,
        cost_estimate=cost(4 * 256 * 256, 1 << 19),
        name="sum_terms",
    )(place, *terms)


def shared_keys(kv):
    beside = swap_z(kv, 1)
    return kv, other_core(kv), beside, other_core(beside)


def body(encoded, span_lens, kv_weight, queries, out_weight, residual):
    span, tp = lax.axis_index("span"), lax.axis_index("tp")
    place = jnp.stack(
        [lax.axis_index("doc"), tp // 2, tp % 2, span // 2, span % 2]
    ).astype(jnp.int32)
    weight = kv_weight.reshape(kv_weight.shape[0], 2 * HD)
    weights = lax.all_gather(out_weight[0], "doc", axis=0)

    swapped = other_half(encoded)
    near = [encoded] + [from_x(encoded, k) for k in (1, 2, 3)]
    row_q, _ = lax.optimization_barrier((queries.reshape(queries.shape[0], GROUP * HD), swapped))
    row_q = jnp.concatenate([row_q, swap_z(row_q, 2)], axis=0)
    all_q = [row_q] + [from_y(row_q, k) for k in (1, 2, 3)]
    far = [swapped] + [from_x(swapped, k) for k in (1, 2, 3)]

    kv_near = shared_keys(project(False, place, span_lens, near, weight))
    carries = attend_near(all_q, kv_near)
    kv_far = project(True, place, span_lens, far, weight)
    beside = swap_z(kv_far, 1)
    beside, carries = lax.optimization_barrier((beside, carries))
    kv_far = kv_far, other_core(kv_far), beside, other_core(beside)

    parts = [None] * 4
    for k in (2, 1, 3, 0):
        part = attend_far(k, place, carries, kv_far)
        parts[k] = from_y(part, -k) if k else part

    joint = fold(64, parts)
    own = fold(64, (joint, swap_z(joint, 2)), last=True)
    beside = swap_z(own, 1)
    other = other_core(jnp.concatenate([own, beside], axis=0))
    terms = output_terms(place, own, beside, other, weights)
    terms = [
        move(term, lambda y, z, c, x, h, j=j: (y + j, z, c, x + y, h))
        for j, term in enumerate(terms)
    ]
    mine, other = sum_terms(place, terms)
    other = other_half(other).astype(f32)
    return (residual.astype(f32) + (mine + other)).astype(bf16)


def solution(mesh):
    placed = (
        P(("doc", "span", "tp"), None),
        P(("doc", "span")),
        P(None, "tp", None),
        P(("doc", "span"), "tp", None),
        P("tp", None, ("doc", "span")),
        P("tp", ("doc", "span")),
    )
    return jax.shard_map(
        body, mesh=mesh, in_specs=placed, out_specs=P("tp", ("doc", "span")), check_vma=False
    )
```

profile of v0, /device:TPU:8, one launch (start us, length us, event | category | flops | bytes accessed | tf_op | source)
XLA Modules:
  0.0 133.1 jit_solution(9308038410135055748)
XLA Ops:
  6.5 0.7 all-gather.2.cloned.1.call-update
  7.3 3.1 %collective-permute-start.10 = (bf16[128,1024]{1,0:T(8,128)(2,1)}, bf16[128,1024]{1,0:T(8,128)(2,1)S(1)}, u32[]{:S(2)}, u32[]{:S(2)}) collective-permute-start(bf16[128,1024]{1,0:T(8,128)(2,1)} %e0.1), channel_id=1, source_target_pairs={{0,4},{1,5},{2,6},{3,7},{4,0},{5,1},{6,2},{7,3},{8,12},{9,13},{10,... | collective-permute-start | bytes 786440 | tf_op jit(solution)/shard_map/ppermute | solution.py:31
  10.4 0.6 collective-permute-start.11
  11.0 2.6 %collective-permute-start.9 = (bf16[128,1024]{1,0:T(8,128)(2,1)}, bf16[128,1024]{1,0:T(8,128)(2,1)S(1)}, u32[]{:S(2)}, u32[]{:S(2)}) collective-permute-start(bf16[128,1024]{1,0:T(8,128)(2,1)} %e0.1), channel_id=1, source_target_pairs={{0,6},{1,7},{2,0},{3,1},{4,2},{5,3},{6,4},{7,5},{8,14},{9,15},{10,... | collective-permute-start | bytes 786440 | tf_op jit(solution)/shard_map/ppermute | solution.py:31
  13.6 7.2 %collective-permute-start = (bf16[128,1024]{1,0:T(8,128)(2,1)}, bf16[128,1024]{1,0:T(8,128)(2,1)S(1)}, u32[]{:S(2)}, u32[]{:S(2)}) collective-permute-start(bf16[128,1024]{1,0:T(8,128)(2,1)} %e0.1), channel_id=1, source_target_pairs={{0,1},{1,0},{2,3},{3,2},{4,5},{5,4},{6,7},{7,6},{8,9},{9,8},{10,11... | collective-permute-start | bytes 786440 | tf_op jit(solution)/shard_map/ppermute | solution.py:31
  20.9 1.8 %collective-permute-done.11.e3 = bf16[128,1024]{1,0:T(8,128)(2,1)S(1)} collective-permute-done((bf16[128,1024]{1,0:T(8,128)(2,1)}, bf16[128,1024]{1,0:T(8,128)(2,1)S(1)}, u32[]{:S(2)}, u32[]{:S(2)}) %collective-permute-start.11) | collective-permute-done | bytes 262176 | tf_op jit(solution)/shard_map/ppermute | solution.py:31
  22.9 1.1 copy-done
  23.9 1.0 copy-done.3
  24.9 0.7 copy-done.4
  25.6 1.0 project.3.n0
  26.6 2.0 %collective-permute-start.13 = (bf16[528,256]{1,0:T(8,128)(2,1)S(1)}, bf16[528,256]{1,0:T(8,128)(2,1)S(1)}, u32[]{:S(2)}, u32[]{:S(2)}) collective-permute-start(bf16[528,256]{1,0:T(8,128)(2,1)S(1)} %project.3.n0), channel_id=1, source_target_pairs={{0,16},{1,17},{2,18},{3,19},{4,20},{5,21},{6,22},{7,23},{8,24},{9,... | collective-permute-start | bytes 811016 | tf_op jit(solution)/shard_map/ppermute | solution.py:31
  28.6 5.8 %collective-permute-start.5 = (bf16[32,1024]{1,0:T(8,128)(2,1)S(1)}, bf16[32,1024]{1,0:T(8,128)(2,1)S(1)}, u32[]{:S(2)}, u32[]{:S(2)}) collective-permute-start(bf16[32,1024]{1,0:T(8,128)(2,1)S(1)} %bitcast.9), channel_id=1, source_target_pairs={{0,32},{1,33},{2,34},{3,35},{4,36},{5,37},{6,38},{7,39},{8,40},{9,... | collective-permute-start | bytes 196616 | tf_op jit(solution)/shard_map/ppermute | solution.py:31
  34.5 1.0 collective-permute-start.2
  35.5 0.9 collective-permute-start.3
  36.4 1.4 %collective-permute-done.5 = bf16[32,1024]{1,0:T(8,128)(2,1)S(1)} collective-permute-done((bf16[32,1024]{1,0:T(8,128)(2,1)S(1)}, bf16[32,1024]{1,0:T(8,128)(2,1)S(1)}, u32[]{:S(2)}, u32[]{:S(2)}) %collective-permute-start.5) | collective-permute-done | bytes 65568 | tf_op jit(solution)/shard_map/ppermute | solution.py:31
  38.0 2.1 %collective-permute-done.13.n2 = bf16[528,256]{1,0:T(8,128)(2,1)S(1)} collective-permute-done((bf16[528,256]{1,0:T(8,128)(2,1)S(1)}, bf16[528,256]{1,0:T(8,128)(2,1)S(1)}, u32[]{:S(2)}, u32[]{:S(2)}) %collective-permute-start.13) | collective-permute-done | bytes 270368 | tf_op jit(solution)/shard_map/ppermute | solution.py:31
  40.0 3.6 %collective-permute-done.1.e1 = bf16[128,1024]{1,0:T(8,128)(2,1)S(1)} collective-permute-done((bf16[128,1024]{1,0:T(8,128)(2,1)S(1)}, bf16[128,1024]{1,0:T(8,128)(2,1)S(1)}, u32[]{:S(2)}, u32[]{:S(2)}) %collective-permute-start.1) | collective-permute-done | bytes 262176 | tf_op jit(solution)/shard_map/ppermute | solution.py:31
  44.1 1.2 collective-permute-done.2.e2
  45.3 2.3 %collective-permute-start.7 = (bf16[64,1024]{1,0:T(8,128)(2,1)S(1)}, bf16[64,1024]{1,0:T(8,128)(2,1)S(1)}, u32[]{:S(2)}, u32[]{:S(2)}) collective-permute-start(bf16[64,1024]{1,0:T(8,128)(2,1)S(1)} %constant_dynamic-update-slice_fusion.q0), channel_id=1, source_target_pairs={{0,128},{1,129},{2,130},{3,131},{4,132},{5,133},{6,134},{7,135},{8... | collective-permute-start | bytes 393224 | tf_op jit(solution)/shard_map/ppermute | solution.py:31
  47.6 1.4 %collective-permute-done.3.e3 = bf16[128,1024]{1,0:T(8,128)(2,1)S(1)} collective-permute-done((bf16[128,1024]{1,0:T(8,128)(2,1)S(1)}, bf16[128,1024]{1,0:T(8,128)(2,1)S(1)}, u32[]{:S(2)}, u32[]{:S(2)}) %collective-permute-start.3) | collective-permute-done | bytes 262176 | tf_op jit(solution)/shard_map/ppermute | solution.py:31
  49.0 1.6 %collective-permute-start.8 = (bf16[64,1024]{1,0:T(8,128)(2,1)S(1)}, bf16[64,1024]{1,0:T(8,128)(2,1)S(1)}, u32[]{:S(2)}, u32[]{:S(2)}) collective-permute-start(bf16[64,1024]{1,0:T(8,128)(2,1)S(1)} %constant_dynamic-update-slice_fusion.q0), channel_id=1, source_target_pairs={{0,64},{1,65},{2,66},{3,67},{4,68},{5,69},{6,70},{7,71},{8,72},{9,... | collective-permute-start | bytes 393224 | tf_op jit(solution)/shard_map/ppermute | solution.py:31
  50.6 1.0 project.2.n0
  52.1 2.6 %collective-permute-done.8.q3 = bf16[64,1024]{1,0:T(8,128)(2,1)S(1)} collective-permute-done((bf16[64,1024]{1,0:T(8,128)(2,1)S(1)}, bf16[64,1024]{1,0:T(8,128)(2,1)S(1)}, u32[]{:S(2)}, u32[]{:S(2)}) %collective-permute-start.8) | collective-permute-done | bytes 131104 | tf_op jit(solution)/shard_map/ppermute | solution.py:31
  54.7 5.3 %attend_near.1 = (bf16[4,64,1024]{2,1,0:T(8,128)(2,1)S(1)}, f32[4,64,1024]{2,1,0:T(8,128)S(1)}, f32[4,64,128]{2,1,0:T(8,128)S(1)}) custom-call(bf16[64,1024]{1,0:T(8,128)(2,1)S(1)} %constant_dynamic-update-slice_fusion.q0, bf16[64,1024]{1,0:T(8,128)(2,1)S(1)} %collective-permute-done.6.q1, bf16[64,1024]{1,0:T(8,128)(2,1)S(1)} %collective-permute-done.7.q2, ...), custom_call_target="tpu_custom_call" | custom-call | flops 4294967296 | bytes 3145728 | tf_op jit(solution)/shard_map/attend_near/pallas_call | solution.py:204
  60.1 1.5 %collective-permute-done.16.n3 = bf16[528,256]{1,0:T(8,128)(2,1)S(1)} collective-permute-done((bf16[528,256]{1,0:T(8,128)(2,1)S(1)}, bf16[528,256]{1,0:T(8,128)(2,1)S(1)}, u32[]{:S(2)}, u32[]{:S(2)}) %collective-permute-start.16) | collective-permute-done | bytes 270368 | tf_op jit(solution)/shard_map/ppermute | solution.py:31
  61.6 2.4 %attend_far.7 = bf16[80,1024]{1,0:T(8,128)(2,1)S(1)} custom-call(s32[5]{0:T(128)S(1)} %stack.23.place_ref, bf16[4,64,1024]{2,1,0:T(8,128)(2,1)S(1)} %get-tuple-element.23.q_all, bf16[528,256]{1,0:T(8,128)(2,1)S(1)} %project.2.n0, bf16[528,256]{1,0:T(8,128)(2,1)S(1)} %collective-permute-done.15.n1, bf16[528,256]{1,0:T(8,128)(2,1)S(1)} %collective-permute-done.4.n2, ...), custom_call_target="tpu_custom_call" | custom-call | flops 1073741824 | bytes 2097152 | tf_op jit(solution)/shard_map/attend_far/pallas_call | solution.py:237
  64.0 1.7 %collective-permute-start.19 = (bf16[80,1024]{1,0:T(8,128)(2,1)S(1)}, bf16[80,1024]{1,0:T(8,128)(2,1)S(1)}, u32[]{:S(2)}, u32[]{:S(2)}) collective-permute-start(bf16[80,1024]{1,0:T(8,128)(2,1)S(1)} %attend_far.7), channel_id=1, source_target_pairs={{0,192},{1,193},{2,194},{3,195},{4,196},{5,197},{6,198},{7,199},{8... | collective-permute-start | bytes 491528 | tf_op jit(solution)/shard_map/ppermute | solution.py:31
  65.7 2.4 %attend_far.6 = bf16[80,1024]{1,0:T(8,128)(2,1)S(1)} custom-call(s32[5]{0:T(128)S(1)} %stack.23.place_ref, bf16[4,64,1024]{2,1,0:T(8,128)(2,1)S(1)} %get-tuple-element.23.q_all, bf16[528,256]{1,0:T(8,128)(2,1)S(1)} %project.2.n0, bf16[528,256]{1,0:T(8,128)(2,1)S(1)} %collective-permute-done.15.n1, bf16[528,256]{1,0:T(8,128)(2,1)S(1)} %collective-permute-done.4.n2, ...), custom_call_target="tpu_custom_call" | custom-call | flops 1073741824 | bytes 2097152 | tf_op jit(solution)/shard_map/attend_far/pallas_call | solution.py:237
  68.1 1.4 %collective-permute-start.18 = (bf16[80,1024]{1,0:T(8,128)(2,1)S(1)}, bf16[80,1024]{1,0:T(8,128)(2,1)S(1)}, u32[]{:S(2)}, u32[]{:S(2)}) collective-permute-start(bf16[80,1024]{1,0:T(8,128)(2,1)S(1)} %attend_far.6), channel_id=1, source_target_pairs={{0,128},{1,129},{2,130},{3,131},{4,132},{5,133},{6,134},{7,135},{8... | collective-permute-start | bytes 491528 | tf_op jit(solution)/shard_map/ppermute | solution.py:31
  69.5 2.4 %attend_far.5 = bf16[80,1024]{1,0:T(8,128)(2,1)S(1)} custom-call(s32[5]{0:T(128)S(1)} %stack.23.place_ref, bf16[4,64,1024]{2,1,0:T(8,128)(2,1)S(1)} %get-tuple-element.23.q_all, bf16[528,256]{1,0:T(8,128)(2,1)S(1)} %project.2.n0, bf16[528,256]{1,0:T(8,128)(2,1)S(1)} %collective-permute-done.15.n1, bf16[528,256]{1,0:T(8,128)(2,1)S(1)} %collective-permute-done.4.n2, ...), custom_call_target="tpu_custom_call" | custom-call | flops 1073741824 | bytes 2097152 | tf_op jit(solution)/shard_map/attend_far/pallas_call | solution.py:237
  71.9 2.0 %collective-permute-start.17 = (bf16[80,1024]{1,0:T(8,128)(2,1)S(1)}, bf16[80,1024]{1,0:T(8,128)(2,1)S(1)}, u32[]{:S(2)}, u32[]{:S(2)}) collective-permute-start(bf16[80,1024]{1,0:T(8,128)(2,1)S(1)} %attend_far.5), channel_id=1, source_target_pairs={{0,64},{1,65},{2,66},{3,67},{4,68},{5,69},{6,70},{7,71},{8,72},{9,... | collective-permute-start | bytes 491528 | tf_op jit(solution)/shard_map/ppermute | solution.py:31
  73.9 2.4 %attend_far.4.refs_0_ = bf16[80,1024]{1,0:T(8,128)(2,1)S(1)} custom-call(s32[5]{0:T(128)S(1)} %stack.23.place_ref, bf16[4,64,1024]{2,1,0:T(8,128)(2,1)S(1)} %get-tuple-element.23.q_all, bf16[528,256]{1,0:T(8,128)(2,1)S(1)} %project.2.n0, bf16[528,256]{1,0:T(8,128)(2,1)S(1)} %collective-permute-done.15.n1, bf16[528,256]{1,0:T(8,128)(2,1)S(1)} %collective-permute-done.4.n2, ...), custom_call_target="tpu_custom_call" | custom-call | flops 1073741824 | bytes 2097152 | tf_op jit(solution)/shard_map/attend_far/pallas_call | solution.py:237
  76.3 1.8 %collective-permute-done.17.refs_1_ = bf16[80,1024]{1,0:T(8,128)(2,1)S(1)} collective-permute-done((bf16[80,1024]{1,0:T(8,128)(2,1)S(1)}, bf16[80,1024]{1,0:T(8,128)(2,1)S(1)}, u32[]{:S(2)}, u32[]{:S(2)}) %collective-permute-start.17) | collective-permute-done | bytes 163872 | tf_op jit(solution)/shard_map/ppermute | solution.py:31
  78.7 9.3 %collective-permute-done.20.refs_1_ = bf16[80,1024]{1,0:T(8,128)(2,1)S(1)} collective-permute-done((bf16[80,1024]{1,0:T(8,128)(2,1)S(1)}, bf16[80,1024]{1,0:T(8,128)(2,1)S(1)}, u32[]{:S(2)}, u32[]{:S(2)}) %collective-permute-start.20) | collective-permute-done | bytes 163872 | tf_op jit(solution)/shard_map/ppermute | solution.py:31
  88.5 5.1 %collective-permute-done.21.beside = bf16[64,1024]{1,0:T(8,128)(2,1)S(1)} collective-permute-done((bf16[64,1024]{1,0:T(8,128)(2,1)S(1)}, bf16[64,1024]{1,0:T(8,128)(2,1)S(1)}, u32[]{:S(2)}, u32[]{:S(2)}) %collective-permute-start.21) | collective-permute-done | bytes 131104 | tf_op jit(solution)/shard_map/ppermute | solution.py:31
  93.7 1.5 %collective-permute-done.22.other = bf16[128,1024]{1,0:T(8,128)(2,1)S(1)} collective-permute-done((bf16[128,1024]{1,0:T(8,128)(2,1)S(1)}, bf16[128,1024]{1,0:T(8,128)(2,1)S(1)}, u32[]{:S(2)}, u32[]{:S(2)}) %collective-permute-start.22) | collective-permute-done | bytes 262176 | tf_op jit(solution)/shard_map/ppermute | solution.py:31
  95.2 1.6 %copy-done.2 = bf16[4,1024,256]{2,1,0:T(8,128)(2,1)S(1)} copy-done((bf16[4,1024,256]{2,1,0:T(8,128)(2,1)S(1)}, bf16[4,1024,256]{2,1,0:T(8,128)(2,1)}, u32[]{:S(2)}) %copy-start.2) | copy-done | bytes 2097176
  96.8 1.3 output.1
  98.1 3.0 %collective-permute-start.23 = (bf16[256,256]{1,0:T(8,128)(2,1)S(1)}, bf16[256,256]{1,0:T(8,128)(2,1)S(1)}, u32[]{:S(2)}, u32[]{:S(2)}) collective-permute-start(bf16[256,256]{1,0:T(8,128)(2,1)S(1)} %get-tuple-element.27), channel_id=1, source_target_pairs={{0,0},{1,1},{2,2},{3,3},{4,4},{5,5},{6,6},{7,7},{8,8},{9,9},{10,10... | collective-permute-start | bytes 393224 | tf_op jit(solution)/shard_map/ppermute | solution.py:31
  101.1 3.5 %collective-permute-start.24 = (bf16[256,256]{1,0:T(8,128)(2,1)S(1)}, bf16[256,256]{1,0:T(8,128)(2,1)S(1)}, u32[]{:S(2)}, u32[]{:S(2)}) collective-permute-start(bf16[256,256]{1,0:T(8,128)(2,1)S(1)} %get-tuple-element.28), channel_id=1, source_target_pairs={{0,64},{1,65},{2,66},{3,67},{4,68},{5,69},{6,70},{7,71},{8,72},{9,... | collective-permute-start | bytes 393224 | tf_op jit(solution)/shard_map/ppermute | solution.py:31
  104.7 2.6 %collective-permute-start.26 = (bf16[256,256]{1,0:T(8,128)(2,1)S(1)}, bf16[256,256]{1,0:T(8,128)(2,1)S(1)}, u32[]{:S(2)}, u32[]{:S(2)}) collective-permute-start(bf16[256,256]{1,0:T(8,128)(2,1)S(1)} %get-tuple-element.30), channel_id=1, source_target_pairs={{0,192},{1,193},{2,194},{3,195},{4,196},{5,197},{6,198},{7,199},{8... | collective-permute-start | bytes 393224 | tf_op jit(solution)/shard_map/ppermute | solution.py:31
  107.5 0.9 collective-permute-done.24.t1
  108.5 4.9 %collective-permute-done.25.t2 = bf16[256,256]{1,0:T(8,128)(2,1)S(1)} collective-permute-done((bf16[256,256]{1,0:T(8,128)(2,1)S(1)}, bf16[256,256]{1,0:T(8,128)(2,1)S(1)}, u32[]{:S(2)}, u32[]{:S(2)}) %collective-permute-start.25) | collective-permute-done | bytes 131104 | tf_op jit(solution)/shard_map/ppermute | solution.py:31
  113.4 3.3 %collective-permute-done.26.t3 = bf16[256,256]{1,0:T(8,128)(2,1)S(1)} collective-permute-done((bf16[256,256]{1,0:T(8,128)(2,1)S(1)}, bf16[256,256]{1,0:T(8,128)(2,1)S(1)}, u32[]{:S(2)}, u32[]{:S(2)}) %collective-permute-start.26) | collective-permute-done | bytes 131104 | tf_op jit(solution)/shard_map/ppermute | solution.py:31
  116.7 0.6 sum_terms.1
  117.3 5.1 %collective-permute-start.27 = (bf16[128,256]{1,0:T(8,128)(2,1)S(1)}, bf16[128,256]{1,0:T(8,128)(2,1)S(1)}, u32[]{:S(2)}, u32[]{:S(2)}) collective-permute-start(bf16[128,256]{1,0:T(8,128)(2,1)S(1)} %get-tuple-element.32), channel_id=1, source_target_pairs={{0,1},{1,0},{2,3},{3,2},{4,5},{5,4},{6,7},{7,6},{8,9},{9,8},{10,11... | collective-permute-start | bytes 196616 | tf_op jit(solution)/shard_map/ppermute | solution.py:31
  122.5 3.1 %collective-permute-done.27 = bf16[128,256]{1,0:T(8,128)(2,1)S(1)} collective-permute-done((bf16[128,256]{1,0:T(8,128)(2,1)S(1)}, bf16[128,256]{1,0:T(8,128)(2,1)S(1)}, u32[]{:S(2)}, u32[]{:S(2)}) %collective-permute-start.27) | collective-permute-done | bytes 65568 | tf_op jit(solution)/shard_map/ppermute | solution.py:31
  125.6 0.7 add_convert_fusion
  (41 shorter events, 3.2 us)
Async XLA Ops:
  6.5 44.1 %copy-start.1 = (bf16[1024,1,256]{2,0,1:T(8,128)(2,1)S(1)}, bf16[1024,1,256]{2,0,1:T(8,128)(2,1)}, u32[]{:S(2)}) copy-start(bf16[1024,1,256]{2,0,1:T(8,128)(2,1)} %param.8) | copy-start | bytes 1572868
  6.5 22.0 %copy-start.6 = (bf16[32,1,1024]{2,0,1:T(8,128)(2,1)S(1)}, bf16[32,1,1024]{2,0,1:T(8,128)(2,1)}, u32[]{:S(2)}) copy-start(bf16[32,1,1024]{2,0,1:T(8,128)(2,1)} %param.9) | copy-start | bytes 196612
  6.5 88.7 %all-gather.2.cloned.1.call-start = ((), (), s32[]{:S(2)}) async-start(), calls=%async_computation | async-start | bytes 2621440 | tf_op jit(solution)/shard_map/all_gather | solution.py:351
  7.3 13.6 %collective-permute-start.10 = (bf16[128,1024]{1,0:T(8,128)(2,1)}, bf16[128,1024]{1,0:T(8,128)(2,1)S(1)}, u32[]{:S(2)}, u32[]{:S(2)}) collective-permute-start(bf16[128,1024]{1,0:T(8,128)(2,1)} %e0.1), channel_id=1, source_target_pairs={{0,4},{1,5},{2,6},{3,7},{4,0},{5,1},{6,2},{7,3},{8,12},{9,13},{10,... | collective-permute-start | bytes 786440 | tf_op jit(solution)/shard_map/ppermute | solution.py:31
  10.4 12.4 %collective-permute-start.11 = (bf16[128,1024]{1,0:T(8,128)(2,1)}, bf16[128,1024]{1,0:T(8,128)(2,1)S(1)}, u32[]{:S(2)}, u32[]{:S(2)}) collective-permute-start(bf16[128,1024]{1,0:T(8,128)(2,1)} %e0.1), channel_id=1, source_target_pairs={{0,2},{1,3},{2,4},{3,5},{4,6},{5,7},{6,0},{7,1},{8,10},{9,11},{10,... | collective-permute-start | bytes 786440 | tf_op jit(solution)/shard_map/ppermute | solution.py:31
  11.0 11.9 %collective-permute-start.9 = (bf16[128,1024]{1,0:T(8,128)(2,1)}, bf16[128,1024]{1,0:T(8,128)(2,1)S(1)}, u32[]{:S(2)}, u32[]{:S(2)}) collective-permute-start(bf16[128,1024]{1,0:T(8,128)(2,1)} %e0.1), channel_id=1, source_target_pairs={{0,6},{1,7},{2,0},{3,1},{4,2},{5,3},{6,4},{7,5},{8,14},{9,15},{10,... | collective-permute-start | bytes 786440 | tf_op jit(solution)/shard_map/ppermute | solution.py:31
  13.6 15.0 %collective-permute-start = (bf16[128,1024]{1,0:T(8,128)(2,1)}, bf16[128,1024]{1,0:T(8,128)(2,1)S(1)}, u32[]{:S(2)}, u32[]{:S(2)}) collective-permute-start(bf16[128,1024]{1,0:T(8,128)(2,1)} %e0.1), channel_id=1, source_target_pairs={{0,1},{1,0},{2,3},{3,2},{4,5},{5,4},{6,7},{7,6},{8,9},{9,8},{10,11... | collective-permute-start | bytes 786440 | tf_op jit(solution)/shard_map/ppermute | solution.py:31
  22.8 1.1 copy-start
  23.9 1.0 copy-start.3
  24.9 0.7 copy-start.4
  26.6 13.5 %collective-permute-start.13 = (bf16[528,256]{1,0:T(8,128)(2,1)S(1)}, bf16[528,256]{1,0:T(8,128)(2,1)S(1)}, u32[]{:S(2)}, u32[]{:S(2)}) collective-permute-start(bf16[528,256]{1,0:T(8,128)(2,1)S(1)} %project.3.n0), channel_id=1, source_target_pairs={{0,16},{1,17},{2,18},{3,19},{4,20},{5,21},{6,22},{7,23},{8,24},{9,... | collective-permute-start | bytes 811016 | tf_op jit(solution)/shard_map/ppermute | solution.py:31
  28.6 9.2 %collective-permute-start.5 = (bf16[32,1024]{1,0:T(8,128)(2,1)S(1)}, bf16[32,1024]{1,0:T(8,128)(2,1)S(1)}, u32[]{:S(2)}, u32[]{:S(2)}) collective-permute-start(bf16[32,1024]{1,0:T(8,128)(2,1)S(1)} %bitcast.9), channel_id=1, source_target_pairs={{0,32},{1,33},{2,34},{3,35},{4,36},{5,37},{6,38},{7,39},{8,40},{9,... | collective-permute-start | bytes 196616 | tf_op jit(solution)/shard_map/ppermute | solution.py:31
  34.4 9.2 %collective-permute-start.1 = (bf16[128,1024]{1,0:T(8,128)(2,1)S(1)}, bf16[128,1024]{1,0:T(8,128)(2,1)S(1)}, u32[]{:S(2)}, u32[]{:S(2)}) collective-permute-start(bf16[128,1024]{1,0:T(8,128)(2,1)S(1)} %collective-permute-done.e0), channel_id=1, source_target_pairs={{0,6},{1,7},{2,0},{3,1},{4,2},{5,3},{6,4},{7,5},{8,14},{9,15},{10,... | collective-permute-start | bytes 786440 | tf_op jit(solution)/shard_map/ppermute | solution.py:31
  34.5 10.8 %collective-permute-start.2 = (bf16[128,1024]{1,0:T(8,128)(2,1)S(1)}, bf16[128,1024]{1,0:T(8,128)(2,1)S(1)}, u32[]{:S(2)}, u32[]{:S(2)}) collective-permute-start(bf16[128,1024]{1,0:T(8,128)(2,1)S(1)} %collective-permute-done.e0), channel_id=1, source_target_pairs={{0,4},{1,5},{2,6},{3,7},{4,0},{5,1},{6,2},{7,3},{8,12},{9,13},{10,... | collective-permute-start | bytes 786440 | tf_op jit(solution)/shard_map/ppermute | solution.py:31
  35.5 13.5 %collective-permute-start.3 = (bf16[128,1024]{1,0:T(8,128)(2,1)S(1)}, bf16[128,1024]{1,0:T(8,128)(2,1)S(1)}, u32[]{:S(2)}, u32[]{:S(2)}) collective-permute-start(bf16[128,1024]{1,0:T(8,128)(2,1)S(1)} %collective-permute-done.e0), channel_id=1, source_target_pairs={{0,2},{1,3},{2,4},{3,5},{4,6},{5,7},{6,0},{7,1},{8,10},{9,11},{10,... | collective-permute-start | bytes 786440 | tf_op jit(solution)/shard_map/ppermute | solution.py:31
  37.8 16.9 %collective-permute-start.12 = (bf16[528,256]{1,0:T(8,128)(2,1)S(1)}, bf16[528,256]{1,0:T(8,128)(2,1)S(1)}, u32[]{:S(2)}, u32[]{:S(2)}) collective-permute-start(bf16[528,256]{1,0:T(8,128)(2,1)S(1)} %project.3.n0), channel_id=1, source_target_pairs={{0,8},{1,9},{2,10},{3,11},{4,12},{5,13},{6,14},{7,15},{8,0},{9,1},... | collective-permute-start | bytes 811016 | tf_op jit(solution)/shard_map/ppermute | solution.py:31
  40.0 14.7 %collective-permute-start.14 = (bf16[528,256]{1,0:T(8,128)(2,1)S(1)}, bf16[528,256]{1,0:T(8,128)(2,1)S(1)}, u32[]{:S(2)}, u32[]{:S(2)}) collective-permute-start(bf16[528,256]{1,0:T(8,128)(2,1)S(1)} %collective-permute-done.13.n2), channel_id=1, source_target_pairs={{0,8},{1,9},{2,10},{3,11},{4,12},{5,13},{6,14},{7,15},{8,0},{9,1},... | collective-permute-start | bytes 811016 | tf_op jit(solution)/shard_map/ppermute | solution.py:31
  43.6 8.0 %collective-permute-start.6 = (bf16[64,1024]{1,0:T(8,128)(2,1)S(1)}, bf16[64,1024]{1,0:T(8,128)(2,1)S(1)}, u32[]{:S(2)}, u32[]{:S(2)}) collective-permute-start(bf16[64,1024]{1,0:T(8,128)(2,1)S(1)} %constant_dynamic-update-slice_fusion.q0), channel_id=1, source_target_pairs={{0,192},{1,193},{2,194},{3,195},{4,196},{5,197},{6,198},{7,199},{8... | collective-permute-start | bytes 393224 | tf_op jit(solution)/shard_map/ppermute | solution.py:31
  45.3 6.8 %collective-permute-start.7 = (bf16[64,1024]{1,0:T(8,128)(2,1)S(1)}, bf16[64,1024]{1,0:T(8,128)(2,1)S(1)}, u32[]{:S(2)}, u32[]{:S(2)}) collective-permute-start(bf16[64,1024]{1,0:T(8,128)(2,1)S(1)} %constant_dynamic-update-slice_fusion.q0), channel_id=1, source_target_pairs={{0,128},{1,129},{2,130},{3,131},{4,132},{5,133},{6,134},{7,135},{8... | collective-permute-start | bytes 393224 | tf_op jit(solution)/shard_map/ppermute | solution.py:31
  49.0 5.7 %collective-permute-start.8 = (bf16[64,1024]{1,0:T(8,128)(2,1)S(1)}, bf16[64,1024]{1,0:T(8,128)(2,1)S(1)}, u32[]{:S(2)}, u32[]{:S(2)}) collective-permute-start(bf16[64,1024]{1,0:T(8,128)(2,1)S(1)} %constant_dynamic-update-slice_fusion.q0), channel_id=1, source_target_pairs={{0,64},{1,65},{2,66},{3,67},{4,68},{5,69},{6,70},{7,71},{8,72},{9,... | collective-permute-start | bytes 393224 | tf_op jit(solution)/shard_map/ppermute | solution.py:31
  51.6 8.4 %collective-permute-start.4 = (bf16[528,256]{1,0:T(8,128)(2,1)S(1)}, bf16[528,256]{1,0:T(8,128)(2,1)S(1)}, u32[]{:S(2)}, u32[]{:S(2)}) collective-permute-start(bf16[528,256]{1,0:T(8,128)(2,1)S(1)} %project.2.n0), channel_id=1, source_target_pairs={{0,16},{1,17},{2,18},{3,19},{4,20},{5,21},{6,22},{7,23},{8,24},{9,... | collective-permute-start | bytes 811016 | tf_op jit(solution)/shard_map/ppermute | solution.py:31
  52.1 8.0 %collective-permute-start.15 = (bf16[528,256]{1,0:T(8,128)(2,1)S(1)}, bf16[528,256]{1,0:T(8,128)(2,1)S(1)}, u32[]{:S(2)}, u32[]{:S(2)}) collective-permute-start(bf16[528,256]{1,0:T(8,128)(2,1)S(1)} %project.2.n0), channel_id=1, source_target_pairs={{0,8},{1,9},{2,10},{3,11},{4,12},{5,13},{6,14},{7,15},{8,0},{9,1},... | collective-permute-start | bytes 811016 | tf_op jit(solution)/shard_map/ppermute | solution.py:31
  60.0 1.6 %collective-permute-start.16 = (bf16[528,256]{1,0:T(8,128)(2,1)S(1)}, bf16[528,256]{1,0:T(8,128)(2,1)S(1)}, u32[]{:S(2)}, u32[]{:S(2)}) collective-permute-start(bf16[528,256]{1,0:T(8,128)(2,1)S(1)} %collective-permute-done.4.n2), channel_id=1, source_target_pairs={{0,8},{1,9},{2,10},{3,11},{4,12},{5,13},{6,14},{7,15},{8,0},{9,1},... | collective-permute-start | bytes 811016 | tf_op jit(solution)/shard_map/ppermute | solution.py:31
  64.0 12.2 %collective-permute-start.19 = (bf16[80,1024]{1,0:T(8,128)(2,1)S(1)}, bf16[80,1024]{1,0:T(8,128)(2,1)S(1)}, u32[]{:S(2)}, u32[]{:S(2)}) collective-permute-start(bf16[80,1024]{1,0:T(8,128)(2,1)S(1)} %attend_far.7), channel_id=1, source_target_pairs={{0,192},{1,193},{2,194},{3,195},{4,196},{5,197},{6,198},{7,199},{8... | collective-permute-start | bytes 491528 | tf_op jit(solution)/shard_map/ppermute | solution.py:31
  68.1 8.2 %collective-permute-start.18 = (bf16[80,1024]{1,0:T(8,128)(2,1)S(1)}, bf16[80,1024]{1,0:T(8,128)(2,1)S(1)}, u32[]{:S(2)}, u32[]{:S(2)}) collective-permute-start(bf16[80,1024]{1,0:T(8,128)(2,1)S(1)} %attend_far.6), channel_id=1, source_target_pairs={{0,128},{1,129},{2,130},{3,131},{4,132},{5,133},{6,134},{7,135},{8... | collective-permute-start | bytes 491528 | tf_op jit(solution)/shard_map/ppermute | solution.py:31
  71.9 6.2 %collective-permute-start.17 = (bf16[80,1024]{1,0:T(8,128)(2,1)S(1)}, bf16[80,1024]{1,0:T(8,128)(2,1)S(1)}, u32[]{:S(2)}, u32[]{:S(2)}) collective-permute-start(bf16[80,1024]{1,0:T(8,128)(2,1)S(1)} %attend_far.5), channel_id=1, source_target_pairs={{0,64},{1,65},{2,66},{3,67},{4,68},{5,69},{6,70},{7,71},{8,72},{9,... | collective-permute-start | bytes 491528 | tf_op jit(solution)/shard_map/ppermute | solution.py:31
  78.5 47.1 %copy-start.5 = (bf16[128,256]{1,0:T(8,128)(2,1)S(1)}, bf16[128,256]{1,0:T(8,128)(2,1)}, u32[]{:S(2)}) copy-start(bf16[128,256]{1,0:T(8,128)(2,1)} %param.11) | copy-start | bytes 196612
  78.5 9.5 %collective-permute-start.20 = (bf16[80,1024]{1,0:T(8,128)(2,1)S(1)}, bf16[80,1024]{1,0:T(8,128)(2,1)S(1)}, u32[]{:S(2)}, u32[]{:S(2)}) collective-permute-start(bf16[80,1024]{1,0:T(8,128)(2,1)S(1)} %fold.2.refs_0_), channel_id=1, source_target_pairs={{0,32},{1,33},{2,34},{3,35},{4,36},{5,37},{6,38},{7,39},{8,40},{9,... | collective-permute-start | bytes 491528 | tf_op jit(solution)/shard_map/ppermute | solution.py:31
  88.4 5.2 %collective-permute-start.21 = (bf16[64,1024]{1,0:T(8,128)(2,1)S(1)}, bf16[64,1024]{1,0:T(8,128)(2,1)S(1)}, u32[]{:S(2)}, u32[]{:S(2)}) collective-permute-start(bf16[64,1024]{1,0:T(8,128)(2,1)S(1)} %fold.3.own), channel_id=1, source_target_pairs={{0,16},{1,17},{2,18},{3,19},{4,20},{5,21},{6,22},{7,23},{8,24},{9,... | collective-permute-start | bytes 393224 | tf_op jit(solution)/shard_map/ppermute | solution.py:31
  93.6 1.6 %collective-permute-start.22 = (bf16[128,1024]{1,0:T(8,128)(2,1)S(1)}, bf16[128,1024]{1,0:T(8,128)(2,1)S(1)}, u32[]{:S(2)}, u32[]{:S(2)}) collective-permute-start(bf16[128,1024]{1,0:T(8,128)(2,1)S(1)} %pad_maximum_fusion), channel_id=1, source_target_pairs={{0,8},{1,9},{2,10},{3,11},{4,12},{5,13},{6,14},{7,15},{8,0},{9,1},... | collective-permute-start | bytes 786440 | tf_op jit(solution)/shard_map/ppermute | solution.py:31
  95.2 1.6 %copy-start.2 = (bf16[4,1024,256]{2,1,0:T(8,128)(2,1)S(1)}, bf16[4,1024,256]{2,1,0:T(8,128)(2,1)}, u32[]{:S(2)}) copy-start(bf16[4,1024,256]{2,1,0:T(8,128)(2,1)} %all-gather.2.cloned.1.call-done.weights) | copy-start | bytes 6291460
  98.1 9.4 %collective-permute-start.23 = (bf16[256,256]{1,0:T(8,128)(2,1)S(1)}, bf16[256,256]{1,0:T(8,128)(2,1)S(1)}, u32[]{:S(2)}, u32[]{:S(2)}) collective-permute-start(bf16[256,256]{1,0:T(8,128)(2,1)S(1)} %get-tuple-element.27), channel_id=1, source_target_pairs={{0,0},{1,1},{2,2},{3,3},{4,4},{5,5},{6,6},{7,7},{8,8},{9,9},{10,10... | collective-permute-start | bytes 393224 | tf_op jit(solution)/shard_map/ppermute | solution.py:31
  101.1 7.4 %collective-permute-start.24 = (bf16[256,256]{1,0:T(8,128)(2,1)S(1)}, bf16[256,256]{1,0:T(8,128)(2,1)S(1)}, u32[]{:S(2)}, u32[]{:S(2)}) collective-permute-start(bf16[256,256]{1,0:T(8,128)(2,1)S(1)} %get-tuple-element.28), channel_id=1, source_target_pairs={{0,64},{1,65},{2,66},{3,67},{4,68},{5,69},{6,70},{7,71},{8,72},{9,... | collective-permute-start | bytes 393224 | tf_op jit(solution)/shard_map/ppermute | solution.py:31
  104.6 8.8 %collective-permute-start.25 = (bf16[256,256]{1,0:T(8,128)(2,1)S(1)}, bf16[256,256]{1,0:T(8,128)(2,1)S(1)}, u32[]{:S(2)}, u32[]{:S(2)}) collective-permute-start(bf16[256,256]{1,0:T(8,128)(2,1)S(1)} %get-tuple-element.29), channel_id=1, source_target_pairs={{0,128},{1,129},{2,130},{3,131},{4,132},{5,133},{6,134},{7,135},{8... | collective-permute-start | bytes 393224 | tf_op jit(solution)/shard_map/ppermute | solution.py:31
  104.7 12.0 %collective-permute-start.26 = (bf16[256,256]{1,0:T(8,128)(2,1)S(1)}, bf16[256,256]{1,0:T(8,128)(2,1)S(1)}, u32[]{:S(2)}, u32[]{:S(2)}) collective-permute-start(bf16[256,256]{1,0:T(8,128)(2,1)S(1)} %get-tuple-element.30), channel_id=1, source_target_pairs={{0,192},{1,193},{2,194},{3,195},{4,196},{5,197},{6,198},{7,199},{8... | collective-permute-start | bytes 393224 | tf_op jit(solution)/shard_map/ppermute | solution.py:31
  117.3 8.3 %collective-permute-start.27 = (bf16[128,256]{1,0:T(8,128)(2,1)S(1)}, bf16[128,256]{1,0:T(8,128)(2,1)S(1)}, u32[]{:S(2)}, u32[]{:S(2)}) collective-permute-start(bf16[128,256]{1,0:T(8,128)(2,1)S(1)} %get-tuple-element.32), channel_id=1, source_target_pairs={{0,1},{1,0},{2,3},{3,2},{4,5},{5,4},{6,7},{7,6},{8,9},{9,8},{10,11... | collective-permute-start | bytes 196616 | tf_op jit(solution)/shard_map/ppermute | solution.py:31
Sparse Core Ops, SparseCore 0:
  9.2 35.8 all-gather.1
where the time goes:
time: 134 us; the launch traced here: 133 us
  starting transfers between devices  48.1 us (36%)
  waiting for transfers between devices  46.7 us (35%)
  Pallas kernels  19.6 us (15%)
  between operations  13.6 us (10%)
  local copies, waits for them, and re-layouts  4.4 us (3%)
    ppermute x28, starting transfers between devices, move(): return lax.ppermute(value, AXES, pairs)  48.1 us
    ppermute x28, waiting for transfers between devices, move(): return lax.ppermute(value, AXES, pairs)  46 us
    pallas_call x4, Pallas kernels, attend_far(): pl.pallas_call(functools.partial(far_kernel, k), out_shape=jax.ShapeDtype...  9.57 us
    pallas_call x1, Pallas kernels, attend_near(): pl.pallas_call(near_kernel, out_shape=(jax.ShapeDtypeStruct((4, count, GR...  5.3 us
    unnamed x15, local copies, waits for them, and re-layouts  4.31 us
  transfers between devices with their start and end apart: 29, of which 18 were waited for; matrix products, arithmetic and copies ran while one was open for 0% of the time, Pallas kernels for 13%

commit v1 on v0

--- a/solution.py
+++ b/solution.py
@@ -99,7 +99,7 @@
         in_specs=[SMEM, SMEM] + vmem(5) + [ANY] * len(after),
         out_specs=vmem(1)[0],
         compiler_params=PARAMS,
-        cost_estimate=cost(2 * 512 * 1024 * 256, 2 << 20),
+        cost_estimate=cost(2 * 512 * 1024 * 256, 2 << 20) if flip else cost(1024, 1024),
         name="project",
     )(place, lens, *blocks, weight, *after)
 
@@ -112,15 +112,19 @@
     return high, middle, low
 
 
-def put_stats(out, at, stats):
-    for i, term in enumerate(split3(stats)):
-        out[at : at + 2 * GROUP, i * HD : (i + 1) * HD] = term
-    out[at : at + 2 * GROUP, 3 * HD :] = jnp.zeros((2 * GROUP, (GROUP - 3) * HD), bf16)
-
-
-def get_stats(part, at):
-    terms = [part[at : at + 2 * GROUP, i * HD : (i + 1) * HD].astype(f32) for i in range(3)]
-    return (terms[0] + terms[1]) + terms[2]
+def put_stats(out, stats):
+    terms = [term.astype(f32) for term in split3(stats)]
+    lane = lax.broadcasted_iota(jnp.int32, stats.shape, 1)
+    for i in (1, 2):
+        shifted = pltpu.roll(terms[i], 2 * GROUP * i, axis=1)
+        terms[0] = jnp.where(lane < 2 * GROUP * i, terms[0], shifted)
+    out[:, GROUP * HD :] = terms[0].astype(bf16)
+
+
+def get_stats(part):
+    terms = part[:, GROUP * HD :].astype(f32)
+    second, third = (pltpu.roll(terms, HD - 2 * GROUP * i, axis=1) for i in (1, 2))
+    return (terms + second) + third
 
 
 def attend_kernel(queries, parts, carries, valued, emit):
@@ -212,7 +216,7 @@
         out_specs=tuple(vmem(3)),
         scratch_shapes=[pltpu.VMEM((2048, 2 * HD), bf16)],
         compiler_params=PARAMS,
-        cost_estimate=cost(4 * 2048 * 2048 * 256, 3 << 20, 2048 * 2048),
+        cost_estimate=cost(1024, 1024),
         name="attend_near",
     )(*queries, *kv)
 
@@ -223,9 +227,8 @@
 
     def emit(i, sums, packed):
         for h, value in enumerate(sums):
-            out[:count, h * HD : (h + 1) * HD] = value.astype(bf16)
-        packed = jnp.concatenate([packed, jnp.zeros((HD - count, HD), f32)], axis=0)
-        put_stats(out, count, packed.T[: 2 * GROUP])
+            out[:, h * HD : (h + 1) * HD] = value.astype(bf16)
+        put_stats(out, packed)
 
     carry = (sums_all.at[at], stats_all[at])
     attend_kernel((q_all.at[at],), (n0, n1, n2, n3), (carry,), valued, emit)
@@ -236,7 +239,7 @@
     count = q_all.shape[1]
     return pl.pallas_call(
         functools.partial(far_kernel, k),
-        out_shape=jax.ShapeDtypeStruct((count + 2 * GROUP, GROUP * HD), bf16),
+        out_shape=jax.ShapeDtypeStruct((count, GROUP * HD + HD), bf16),
         in_specs=[SMEM] + vmem(7),
         out_specs=vmem(1)[0],
         scratch_shapes=[pltpu.VMEM((2048, 2 * HD), bf16)],
@@ -246,41 +249,34 @@
     )(place, q_all, *kv, sums_all, stats_all)
 
 
-def by_rows(array):
-    return jnp.concatenate([array, jnp.zeros((HD - array.shape[0], HD), f32)], axis=0).T
-
-
-def fold_kernel(count, last, *refs):
+def fold_kernel(last, *refs):
     parts, out = refs[:-1], refs[-1]
-    stats = [get_stats(part, count) for part in parts]
-    half = count // 2
+    stats = [get_stats(part) for part in parts]
+    half = out.shape[0] // 2
     if last:
-        lane = lax.broadcasted_iota(jnp.int32, stats[1].shape, 1)
-        ahead, back = (pltpu.roll(stats[1], r, axis=1) for r in (HD - half, half))
-        stats[1] = jnp.where(lane < half, ahead, back)
-    tops = [s[:GROUP] for s in stats]
-    top = functools.reduce(jnp.maximum, tops)
-    factors = [jnp.exp2((t - top) * EXP2_SCALE) for t in tops]
-    total = sum(f * s[GROUP:] for f, s in zip(factors, stats))
-    if last:
-        factors = [f / total for f in factors]
-    else:
-        put_stats(out, count, jnp.concatenate([top, total], axis=0))
-    factors = [by_rows(f)[:count] for f in factors]
+        stats[1] = jnp.concatenate([stats[1][half:], stats[1][:half]], axis=0)
+    top = functools.reduce(jnp.maximum, stats)
+    factors = [jnp.exp2((s - top) * EXP2_SCALE) for s in stats]
+    shifted = [pltpu.roll(f, GROUP, axis=1) for f in factors]
+    total = sum(f * s for f, s in zip(shifted, stats))
+    if not last:
+        lane = lax.broadcasted_iota(jnp.int32, top.shape, 1)
+        put_stats(out, jnp.where(lane < GROUP, top, total))
     for g in range(GROUP):
         lanes = slice(g * HD, (g + 1) * HD)
-        pieces = [part[:count, lanes].astype(f32) for part in parts]
+        pieces = [part[:, lanes].astype(f32) for part in parts]
         if last:
             pieces[1] = jnp.concatenate([pieces[1][half:], pieces[1][:half]], axis=0)
-        out[:count, lanes] = sum(
-            piece * f[:, g : g + 1] for piece, f in zip(pieces, factors)
-        ).astype(bf16)
+        joint = sum(piece * f[:, g : g + 1] for piece, f in zip(pieces, factors))
+        if last:
+            joint = joint / total[:, GROUP + g : GROUP + g + 1]
+        out[:, lanes] = joint.astype(bf16)
 
 
 def fold(count, parts, last=False):
     return pl.pallas_call(
-        functools.partial(fold_kernel, count, last),
-        out_shape=jax.ShapeDtypeStruct((count + (0 if last else 2 * GROUP), GROUP * HD), bf16),
+        functools.partial(fold_kernel, last),
+        out_shape=jax.ShapeDtypeStruct((count, GROUP * HD + (0 if last else HD)), bf16),
         in_specs=vmem(len(parts)),
         out_specs=vmem(1)[0],
         compiler_params=PARAMS,
@@ -337,11 +333,6 @@
     )(place, *terms)
 
 
-def shared_keys(kv):
-    beside = swap_z(kv, 1)
-    return kv, other_core(kv), beside, other_core(beside)
-
-
 def body(encoded, span_lens, kv_weight, queries, out_weight, residual):
     span, tp = lax.axis_index("span"), lax.axis_index("tp")
     place = jnp.stack(
@@ -350,18 +341,21 @@
     weight = kv_weight.reshape(kv_weight.shape[0], 2 * HD)
     weights = lax.all_gather(out_weight[0], "doc", axis=0)
 
+    near = [encoded] + [from_x(encoded, k) for k in (1, 2, 3)]
     swapped = other_half(encoded)
-    near = [encoded] + [from_x(encoded, k) for k in (1, 2, 3)]
-    row_q, _ = lax.optimization_barrier((queries.reshape(queries.shape[0], GROUP * HD), swapped))
+    row_q = queries.reshape(queries.shape[0], GROUP * HD)
     row_q = jnp.concatenate([row_q, swap_z(row_q, 2)], axis=0)
+    far = [swapped] + [from_x(swapped, k) for k in (1, 2, 3)]
     all_q = [row_q] + [from_y(row_q, k) for k in (1, 2, 3)]
-    far = [swapped] + [from_x(swapped, k) for k in (1, 2, 3)]
-
-    kv_near = shared_keys(project(False, place, span_lens, near, weight))
+
+    kv_near = project(False, place, span_lens, near, weight)
+    beside = swap_z(kv_near, 1)
+    kv_near = kv_near, other_core(kv_near), beside, other_core(beside)
     carries = attend_near(all_q, kv_near)
+    far = lax.optimization_barrier(far + all_q)[:4]
     kv_far = project(True, place, span_lens, far, weight)
     beside = swap_z(kv_far, 1)
-    beside, carries = lax.optimization_barrier((beside, carries))
+    beside, carries, weights = lax.optimization_barrier((beside, carries, weights))
     kv_far = kv_far, other_core(kv_far), beside, other_core(beside)
 
     parts = [None] * 4

time: 134 us -> 131 us (0.978)
  starting transfers between devices: 48.1 us -> 44.1 us
  waiting for transfers between devices: 46.7 us -> 48.5 us
  local copies, waits for them, and re-layouts: 4.4 us -> 2.74 us
    ppermute x28, starting transfers between devices: 48.1 us -> 44.1 us  [move(): return lax.ppermute(value, AXES, pairs)]
    ppermute x28, waiting for transfers between devices: 46 us -> 47.8 us  [move(): return lax.ppermute(value, AXES, pairs)]
    unnamed x15 -> x12, local copies, waits for them, and re-layouts: 4.31 us -> 2.66 us
  transfers between devices with their start and end apart: 29 -> 29, of which waited for: 18 -> 15; matrix products, arithmetic and copies ran while one was open for 0% -> 1% of each run, Pallas kernels for 13% -> 11%
where the time goes in v1:
time: 131 us; the launch traced here: 130 us
  waiting for transfers between devices  48.5 us (37%)
  starting transfers between devices  44.1 us (34%)
  Pallas kernels  20 us (15%)
  between operations  13.6 us (10%)
  local copies, waits for them, and re-layouts  2.74 us (2%)
  other arithmetic  1.52 us (1%)
    ppermute x28, waiting for transfers between devices, move(): return lax.ppermute(value, AXES, pairs)  47.8 us
    ppermute x28, starting transfers between devices, move(): return lax.ppermute(value, AXES, pairs)  44.1 us
    pallas_call x4, Pallas kernels, attend_far(): pl.pallas_call(functools.partial(far_kernel, k), out_shape=jax.ShapeDtype...  9.78 us
    pallas_call x1, Pallas kernels, attend_near(): pl.pallas_call(near_kernel, out_shape=(jax.ShapeDtypeStruct((4, count, GR...  5.39 us
    unnamed x12, local copies, waits for them, and re-layouts  2.66 us
  transfers between devices with their start and end apart: 29, of which 15 were waited for; matrix products, arithmetic and copies ran while one was open for 1% of the time, Pallas kernels for 11%

profile of v1, /device:TPU:8, one launch (start us, length us, event | category | flops | bytes accessed | tf_op | source)
XLA Modules:
  0.0 130.4 jit_solution(8850824386205669863)
XLA Ops:
  6.5 0.7 all-gather.2.cloned.1.call-update
  7.3 3.4 %collective-permute-start.4 = (bf16[32,1024]{1,0:T(8,128)(2,1)}, bf16[32,1024]{1,0:T(8,128)(2,1)S(1)}, u32[]{:S(2)}, u32[]{:S(2)}) collective-permute-start(bf16[32,1024]{1,0:T(8,128)(2,1)} %bitcast.9), channel_id=1, source_target_pairs={{0,32},{1,33},{2,34},{3,35},{4,36},{5,37},{6,38},{7,39},{8,40},{9,... | collective-permute-start | bytes 196616 | tf_op jit(solution)/shard_map/ppermute | solution.py:31
  10.6 3.0 %collective-permute-start.10 = (bf16[128,1024]{1,0:T(8,128)(2,1)}, bf16[128,1024]{1,0:T(8,128)(2,1)S(1)}, u32[]{:S(2)}, u32[]{:S(2)}) collective-permute-start(bf16[128,1024]{1,0:T(8,128)(2,1)} %e0.1), channel_id=1, source_target_pairs={{0,4},{1,5},{2,6},{3,7},{4,0},{5,1},{6,2},{7,3},{8,12},{9,13},{10,... | collective-permute-start | bytes 786440 | tf_op jit(solution)/shard_map/ppermute | solution.py:31
  13.6 0.6 collective-permute-start.11
  14.2 2.6 %collective-permute-start.9 = (bf16[128,1024]{1,0:T(8,128)(2,1)}, bf16[128,1024]{1,0:T(8,128)(2,1)S(1)}, u32[]{:S(2)}, u32[]{:S(2)}) collective-permute-start(bf16[128,1024]{1,0:T(8,128)(2,1)} %e0.1), channel_id=1, source_target_pairs={{0,6},{1,7},{2,0},{3,1},{4,2},{5,3},{6,4},{7,5},{8,14},{9,15},{10,... | collective-permute-start | bytes 786440 | tf_op jit(solution)/shard_map/ppermute | solution.py:31
  16.9 5.4 %collective-permute-start = (bf16[128,1024]{1,0:T(8,128)(2,1)}, bf16[128,1024]{1,0:T(8,128)(2,1)S(1)}, u32[]{:S(2)}, u32[]{:S(2)}) collective-permute-start(bf16[128,1024]{1,0:T(8,128)(2,1)} %e0.1), channel_id=1, source_target_pairs={{0,1},{1,0},{2,3},{3,2},{4,5},{5,4},{6,7},{7,6},{8,9},{9,8},{10,11... | collective-permute-start | bytes 786440 | tf_op jit(solution)/shard_map/ppermute | solution.py:31
  22.3 0.8 pad_maximum_fusion.1.q0
  23.1 0.5 collective-permute-start.5
  23.7 2.0 %collective-permute-done.11.e3 = bf16[128,1024]{1,0:T(8,128)(2,1)S(1)} collective-permute-done((bf16[128,1024]{1,0:T(8,128)(2,1)}, bf16[128,1024]{1,0:T(8,128)(2,1)S(1)}, u32[]{:S(2)}, u32[]{:S(2)}) %collective-permute-start.11) | collective-permute-done | bytes 262176 | tf_op jit(solution)/shard_map/ppermute | solution.py:31
  25.8 1.0 copy-done
  26.8 0.9 copy-done.3
  27.8 0.7 copy-done.4
  28.4 1.0 project.3.n0
  29.5 2.0 %collective-permute-start.13 = (bf16[528,256]{1,0:T(8,128)(2,1)S(1)}, bf16[528,256]{1,0:T(8,128)(2,1)S(1)}, u32[]{:S(2)}, u32[]{:S(2)}) collective-permute-start(bf16[528,256]{1,0:T(8,128)(2,1)S(1)} %project.3.n0), channel_id=1, source_target_pairs={{0,16},{1,17},{2,18},{3,19},{4,20},{5,21},{6,22},{7,23},{8,24},{9,... | collective-permute-start | bytes 811016 | tf_op jit(solution)/shard_map/ppermute | solution.py:31
  31.5 2.3 %collective-permute-start.6 = (bf16[64,1024]{1,0:T(8,128)(2,1)S(1)}, bf16[64,1024]{1,0:T(8,128)(2,1)S(1)}, u32[]{:S(2)}, u32[]{:S(2)}) collective-permute-start(bf16[64,1024]{1,0:T(8,128)(2,1)S(1)} %pad_maximum_fusion.1.q0), channel_id=1, source_target_pairs={{0,128},{1,129},{2,130},{3,131},{4,132},{5,133},{6,134},{7,135},{8... | collective-permute-start | bytes 393224 | tf_op jit(solution)/shard_map/ppermute | solution.py:31
  33.8 2.7 %collective-permute-start.1 = (bf16[128,1024]{1,0:T(8,128)(2,1)S(1)}, bf16[128,1024]{1,0:T(8,128)(2,1)S(1)}, u32[]{:S(2)}, u32[]{:S(2)}) collective-permute-start(bf16[128,1024]{1,0:T(8,128)(2,1)S(1)} %collective-permute-done.e0), channel_id=1, source_target_pairs={{0,6},{1,7},{2,0},{3,1},{4,2},{5,3},{6,4},{7,5},{8,14},{9,15},{10,... | collective-permute-start | bytes 786440 | tf_op jit(solution)/shard_map/ppermute | solution.py:31
  36.4 0.9 collective-permute-start.2
  37.3 4.4 %collective-permute-done.6.q2 = bf16[64,1024]{1,0:T(8,128)(2,1)S(1)} collective-permute-done((bf16[64,1024]{1,0:T(8,128)(2,1)S(1)}, bf16[64,1024]{1,0:T(8,128)(2,1)S(1)}, u32[]{:S(2)}, u32[]{:S(2)}) %collective-permute-start.6) | collective-permute-done | bytes 131104 | tf_op jit(solution)/shard_map/ppermute | solution.py:31
  41.7 1.4 %collective-permute-start.7 = (bf16[64,1024]{1,0:T(8,128)(2,1)S(1)}, bf16[64,1024]{1,0:T(8,128)(2,1)S(1)}, u32[]{:S(2)}, u32[]{:S(2)}) collective-permute-start(bf16[64,1024]{1,0:T(8,128)(2,1)S(1)} %pad_maximum_fusion.1.q0), channel_id=1, source_target_pairs={{0,64},{1,65},{2,66},{3,67},{4,68},{5,69},{6,70},{7,71},{8,72},{9,... | collective-permute-start | bytes 393224 | tf_op jit(solution)/shard_map/ppermute | solution.py:31
  43.0 5.4 %collective-permute-done.7.q3 = bf16[64,1024]{1,0:T(8,128)(2,1)S(1)} collective-permute-done((bf16[64,1024]{1,0:T(8,128)(2,1)S(1)}, bf16[64,1024]{1,0:T(8,128)(2,1)S(1)}, u32[]{:S(2)}, u32[]{:S(2)}) %collective-permute-start.7) | collective-permute-done | bytes 131104 | tf_op jit(solution)/shard_map/ppermute | solution.py:31
  48.4 2.4 %collective-permute-done.3.e3 = bf16[128,1024]{1,0:T(8,128)(2,1)S(1)} collective-permute-done((bf16[128,1024]{1,0:T(8,128)(2,1)S(1)}, bf16[128,1024]{1,0:T(8,128)(2,1)S(1)}, u32[]{:S(2)}, u32[]{:S(2)}) %collective-permute-start.3) | collective-permute-done | bytes 262176 | tf_op jit(solution)/shard_map/ppermute | solution.py:31
  50.8 1.0 project.2.n0
  52.7 5.4 %attend_near.1 = (bf16[4,64,1024]{2,1,0:T(8,128)(2,1)S(1)}, f32[4,64,1024]{2,1,0:T(8,128)S(1)}, f32[4,64,128]{2,1,0:T(8,128)S(1)}) custom-call(bf16[64,1024]{1,0:T(8,128)(2,1)S(1)} %pad_maximum_fusion.1.q0, bf16[64,1024]{1,0:T(8,128)(2,1)S(1)} %collective-permute-done.5.q1, bf16[64,1024]{1,0:T(8,128)(2,1)S(1)} %collective-permute-done.6.q2, ...), custom_call_target="tpu_custom_call" | custom-call | flops 1024 | bytes 1024 | tf_op jit(solution)/shard_map/attend_near/pallas_call | solution.py:208
  58.1 2.7 %collective-permute-done.8.n2 = bf16[528,256]{1,0:T(8,128)(2,1)S(1)} collective-permute-done((bf16[528,256]{1,0:T(8,128)(2,1)S(1)}, bf16[528,256]{1,0:T(8,128)(2,1)S(1)}, u32[]{:S(2)}, u32[]{:S(2)}) %collective-permute-start.8) | collective-permute-done | bytes 270368 | tf_op jit(solution)/shard_map/ppermute | solution.py:31
  60.8 1.5 %collective-permute-done.16.n3 = bf16[528,256]{1,0:T(8,128)(2,1)S(1)} collective-permute-done((bf16[528,256]{1,0:T(8,128)(2,1)S(1)}, bf16[528,256]{1,0:T(8,128)(2,1)S(1)}, u32[]{:S(2)}, u32[]{:S(2)}) %collective-permute-start.16) | collective-permute-done | bytes 270368 | tf_op jit(solution)/shard_map/ppermute | solution.py:31
  62.3 2.4 %attend_far.7 = bf16[64,1152]{1,0:T(8,128)(2,1)S(1)} custom-call(s32[5]{0:T(128)S(1)} %stack.23.place_ref, bf16[4,64,1024]{2,1,0:T(8,128)(2,1)S(1)} %get-tuple-element.30.q_all, bf16[528,256]{1,0:T(8,128)(2,1)S(1)} %project.2.n0, bf16[528,256]{1,0:T(8,128)(2,1)S(1)} %collective-permute-done.15.n1, bf16[528,256]{1,0:T(8,128)(2,1)S(1)} %collective-permute-done.8.n2, ...), custom_call_target="tpu_custom_call" | custom-call | flops 1073741824 | bytes 2097152 | tf_op jit(solution)/shard_map/attend_far/pallas_call | solution.py:240
  64.8 1.4 %collective-permute-start.19 = (bf16[64,1152]{1,0:T(8,128)(2,1)S(1)}, bf16[64,1152]{1,0:T(8,128)(2,1)S(1)}, u32[]{:S(2)}, u32[]{:S(2)}) collective-permute-start(bf16[64,1152]{1,0:T(8,128)(2,1)S(1)} %attend_far.7), channel_id=1, source_target_pairs={{0,192},{1,193},{2,194},{3,195},{4,196},{5,197},{6,198},{7,199},{8... | collective-permute-start | bytes 442376 | tf_op jit(solution)/shard_map/ppermute | solution.py:31
  66.2 2.4 %attend_far.6 = bf16[64,1152]{1,0:T(8,128)(2,1)S(1)} custom-call(s32[5]{0:T(128)S(1)} %stack.23.place_ref, bf16[4,64,1024]{2,1,0:T(8,128)(2,1)S(1)} %get-tuple-element.30.q_all, bf16[528,256]{1,0:T(8,128)(2,1)S(1)} %project.2.n0, bf16[528,256]{1,0:T(8,128)(2,1)S(1)} %collective-permute-done.15.n1, bf16[528,256]{1,0:T(8,128)(2,1)S(1)} %collective-permute-done.8.n2, ...), custom_call_target="tpu_custom_call" | custom-call | flops 1073741824 | bytes 2097152 | tf_op jit(solution)/shard_map/attend_far/pallas_call | solution.py:240
  68.8 2.4 %attend_far.5 = bf16[64,1152]{1,0:T(8,128)(2,1)S(1)} custom-call(s32[5]{0:T(128)S(1)} %stack.23.place_ref, bf16[4,64,1024]{2,1,0:T(8,128)(2,1)S(1)} %get-tuple-element.30.q_all, bf16[528,256]{1,0:T(8,128)(2,1)S(1)} %project.2.n0, bf16[528,256]{1,0:T(8,128)(2,1)S(1)} %collective-permute-done.15.n1, bf16[528,256]{1,0:T(8,128)(2,1)S(1)} %collective-permute-done.8.n2, ...), custom_call_target="tpu_custom_call" | custom-call | flops 1073741824 | bytes 2097152 | tf_op jit(solution)/shard_map/attend_far/pallas_call | solution.py:240
  71.2 2.8 %collective-permute-start.17 = (bf16[64,1152]{1,0:T(8,128)(2,1)S(1)}, bf16[64,1152]{1,0:T(8,128)(2,1)S(1)}, u32[]{:S(2)}, u32[]{:S(2)}) collective-permute-start(bf16[64,1152]{1,0:T(8,128)(2,1)S(1)} %attend_far.5), channel_id=1, source_target_pairs={{0,64},{1,65},{2,66},{3,67},{4,68},{5,69},{6,70},{7,71},{8,72},{9,... | collective-permute-start | bytes 442376 | tf_op jit(solution)/shard_map/ppermute | solution.py:31
  74.0 2.4 %attend_far.4.refs_0_ = bf16[64,1152]{1,0:T(8,128)(2,1)S(1)} custom-call(s32[5]{0:T(128)S(1)} %stack.23.place_ref, bf16[4,64,1024]{2,1,0:T(8,128)(2,1)S(1)} %get-tuple-element.30.q_all, bf16[528,256]{1,0:T(8,128)(2,1)S(1)} %project.2.n0, bf16[528,256]{1,0:T(8,128)(2,1)S(1)} %collective-permute-done.15.n1, bf16[528,256]{1,0:T(8,128)(2,1)S(1)} %collective-permute-done.8.n2, ...), custom_call_target="tpu_custom_call" | custom-call | flops 1073741824 | bytes 2097152 | tf_op jit(solution)/shard_map/attend_far/pallas_call | solution.py:240
  76.5 1.7 %collective-permute-done.17.refs_1_ = bf16[64,1152]{1,0:T(8,128)(2,1)S(1)} collective-permute-done((bf16[64,1152]{1,0:T(8,128)(2,1)S(1)}, bf16[64,1152]{1,0:T(8,128)(2,1)S(1)}, u32[]{:S(2)}, u32[]{:S(2)}) %collective-permute-start.17) | collective-permute-done | bytes 147488 | tf_op jit(solution)/shard_map/ppermute | solution.py:31
  78.8 0.7 collective-permute-start.20
  79.4 8.0 %collective-permute-done.20.refs_1_ = bf16[64,1152]{1,0:T(8,128)(2,1)S(1)} collective-permute-done((bf16[64,1152]{1,0:T(8,128)(2,1)S(1)}, bf16[64,1152]{1,0:T(8,128)(2,1)S(1)}, u32[]{:S(2)}, u32[]{:S(2)}) %collective-permute-start.20) | collective-permute-done | bytes 147488 | tf_op jit(solution)/shard_map/ppermute | solution.py:31
  87.9 5.0 %collective-permute-done.21.beside = bf16[64,1024]{1,0:T(8,128)(2,1)S(1)} collective-permute-done((bf16[64,1024]{1,0:T(8,128)(2,1)S(1)}, bf16[64,1024]{1,0:T(8,128)(2,1)S(1)}, u32[]{:S(2)}, u32[]{:S(2)}) %collective-permute-start.21) | collective-permute-done | bytes 131104 | tf_op jit(solution)/shard_map/ppermute | solution.py:31
  93.0 1.5 %collective-permute-done.22.other = bf16[128,1024]{1,0:T(8,128)(2,1)S(1)} collective-permute-done((bf16[128,1024]{1,0:T(8,128)(2,1)S(1)}, bf16[128,1024]{1,0:T(8,128)(2,1)S(1)}, u32[]{:S(2)}, u32[]{:S(2)}) %collective-permute-start.22) | collective-permute-done | bytes 262176 | tf_op jit(solution)/shard_map/ppermute | solution.py:31
  94.5 1.3 output.1
  95.8 1.9 %collective-permute-start.23 = (bf16[256,256]{1,0:T(8,128)(2,1)S(1)}, bf16[256,256]{1,0:T(8,128)(2,1)S(1)}, u32[]{:S(2)}, u32[]{:S(2)}) collective-permute-start(bf16[256,256]{1,0:T(8,128)(2,1)S(1)} %get-tuple-element.35), channel_id=1, source_target_pairs={{0,0},{1,1},{2,2},{3,3},{4,4},{5,5},{6,6},{7,7},{8,8},{9,9},{10,10... | collective-permute-start | bytes 393224 | tf_op jit(solution)/shard_map/ppermute | solution.py:31
  97.7 3.2 %collective-permute-start.24 = (bf16[256,256]{1,0:T(8,128)(2,1)S(1)}, bf16[256,256]{1,0:T(8,128)(2,1)S(1)}, u32[]{:S(2)}, u32[]{:S(2)}) collective-permute-start(bf16[256,256]{1,0:T(8,128)(2,1)S(1)} %get-tuple-element.36), channel_id=1, source_target_pairs={{0,64},{1,65},{2,66},{3,67},{4,68},{5,69},{6,70},{7,71},{8,72},{9,... | collective-permute-start | bytes 393224 | tf_op jit(solution)/shard_map/ppermute | solution.py:31
  100.9 0.9 collective-permute-start.25
  101.8 2.3 %collective-permute-start.26 = (bf16[256,256]{1,0:T(8,128)(2,1)S(1)}, bf16[256,256]{1,0:T(8,128)(2,1)S(1)}, u32[]{:S(2)}, u32[]{:S(2)}) collective-permute-start(bf16[256,256]{1,0:T(8,128)(2,1)S(1)} %get-tuple-element.38), channel_id=1, source_target_pairs={{0,192},{1,193},{2,194},{3,195},{4,196},{5,197},{6,198},{7,199},{8... | collective-permute-start | bytes 393224 | tf_op jit(solution)/shard_map/ppermute | solution.py:31
  104.2 0.9 collective-permute-done.23.t0
  105.1 5.9 %collective-permute-done.25.t2 = bf16[256,256]{1,0:T(8,128)(2,1)S(1)} collective-permute-done((bf16[256,256]{1,0:T(8,128)(2,1)S(1)}, bf16[256,256]{1,0:T(8,128)(2,1)S(1)}, u32[]{:S(2)}, u32[]{:S(2)}) %collective-permute-start.25) | collective-permute-done | bytes 131104 | tf_op jit(solution)/shard_map/ppermute | solution.py:31
  111.0 3.0 %collective-permute-done.26.t3 = bf16[256,256]{1,0:T(8,128)(2,1)S(1)} collective-permute-done((bf16[256,256]{1,0:T(8,128)(2,1)S(1)}, bf16[256,256]{1,0:T(8,128)(2,1)S(1)}, u32[]{:S(2)}, u32[]{:S(2)}) %collective-permute-start.26) | collective-permute-done | bytes 131104 | tf_op jit(solution)/shard_map/ppermute | solution.py:31
  114.0 0.6 sum_terms.1
  114.6 4.9 %collective-permute-start.27 = (bf16[128,256]{1,0:T(8,128)(2,1)S(1)}, bf16[128,256]{1,0:T(8,128)(2,1)S(1)}, u32[]{:S(2)}, u32[]{:S(2)}) collective-permute-start(bf16[128,256]{1,0:T(8,128)(2,1)S(1)} %get-tuple-element.40), channel_id=1, source_target_pairs={{0,1},{1,0},{2,3},{3,2},{4,5},{5,4},{6,7},{7,6},{8,9},{9,8},{10,11... | collective-permute-start | bytes 196616 | tf_op jit(solution)/shard_map/ppermute | solution.py:31
  119.5 3.3 %collective-permute-done.27 = bf16[128,256]{1,0:T(8,128)(2,1)S(1)} collective-permute-done((bf16[128,256]{1,0:T(8,128)(2,1)S(1)}, bf16[128,256]{1,0:T(8,128)(2,1)S(1)}, u32[]{:S(2)}, u32[]{:S(2)}) %collective-permute-start.27) | collective-permute-done | bytes 65568 | tf_op jit(solution)/shard_map/ppermute | solution.py:31
  122.9 0.7 add_convert_fusion
  (38 shorter events, 2.3 us)
Async XLA Ops:
  6.5 44.3 %copy-start.1 = (bf16[1024,1,256]{2,0,1:T(8,128)(2,1)S(1)}, bf16[1024,1,256]{2,0,1:T(8,128)(2,1)}, u32[]{:S(2)}) copy-start(bf16[1024,1,256]{2,0,1:T(8,128)(2,1)} %param.8) | copy-start | bytes 1572868
  6.5 54.3 %all-gather.2.cloned.1.call-start = ((), (), s32[]{:S(2)}) async-start(), calls=%async_computation | async-start | bytes 2621440 | tf_op jit(solution)/shard_map/all_gather | solution.py:342
  7.3 15.0 %collective-permute-start.4 = (bf16[32,1024]{1,0:T(8,128)(2,1)}, bf16[32,1024]{1,0:T(8,128)(2,1)S(1)}, u32[]{:S(2)}, u32[]{:S(2)}) collective-permute-start(bf16[32,1024]{1,0:T(8,128)(2,1)} %bitcast.9), channel_id=1, source_target_pairs={{0,32},{1,33},{2,34},{3,35},{4,36},{5,37},{6,38},{7,39},{8,40},{9,... | collective-permute-start | bytes 196616 | tf_op jit(solution)/shard_map/ppermute | solution.py:31
  10.6 13.1 %collective-permute-start.10 = (bf16[128,1024]{1,0:T(8,128)(2,1)}, bf16[128,1024]{1,0:T(8,128)(2,1)S(1)}, u32[]{:S(2)}, u32[]{:S(2)}) collective-permute-start(bf16[128,1024]{1,0:T(8,128)(2,1)} %e0.1), channel_id=1, source_target_pairs={{0,4},{1,5},{2,6},{3,7},{4,0},{5,1},{6,2},{7,3},{8,12},{9,13},{10,... | collective-permute-start | bytes 786440 | tf_op jit(solution)/shard_map/ppermute | solution.py:31
  13.6 12.1 %collective-permute-start.11 = (bf16[128,1024]{1,0:T(8,128)(2,1)}, bf16[128,1024]{1,0:T(8,128)(2,1)S(1)}, u32[]{:S(2)}, u32[]{:S(2)}) collective-permute-start(bf16[128,1024]{1,0:T(8,128)(2,1)} %e0.1), channel_id=1, source_target_pairs={{0,2},{1,3},{2,4},{3,5},{4,6},{5,7},{6,0},{7,1},{8,10},{9,11},{10,... | collective-permute-start | bytes 786440 | tf_op jit(solution)/shard_map/ppermute | solution.py:31
  14.2 11.6 %collective-permute-start.9 = (bf16[128,1024]{1,0:T(8,128)(2,1)}, bf16[128,1024]{1,0:T(8,128)(2,1)S(1)}, u32[]{:S(2)}, u32[]{:S(2)}) collective-permute-start(bf16[128,1024]{1,0:T(8,128)(2,1)} %e0.1), channel_id=1, source_target_pairs={{0,6},{1,7},{2,0},{3,1},{4,2},{5,3},{6,4},{7,5},{8,14},{9,15},{10,... | collective-permute-start | bytes 786440 | tf_op jit(solution)/shard_map/ppermute | solution.py:31
  16.9 16.9 %collective-permute-start = (bf16[128,1024]{1,0:T(8,128)(2,1)}, bf16[128,1024]{1,0:T(8,128)(2,1)S(1)}, u32[]{:S(2)}, u32[]{:S(2)}) collective-permute-start(bf16[128,1024]{1,0:T(8,128)(2,1)} %e0.1), channel_id=1, source_target_pairs={{0,1},{1,0},{2,3},{3,2},{4,5},{5,4},{6,7},{7,6},{8,9},{9,8},{10,11... | collective-permute-start | bytes 786440 | tf_op jit(solution)/shard_map/ppermute | solution.py:31
  23.1 14.2 %collective-permute-start.5 = (bf16[64,1024]{1,0:T(8,128)(2,1)S(1)}, bf16[64,1024]{1,0:T(8,128)(2,1)S(1)}, u32[]{:S(2)}, u32[]{:S(2)}) collective-permute-start(bf16[64,1024]{1,0:T(8,128)(2,1)S(1)} %pad_maximum_fusion.1.q0), channel_id=1, source_target_pairs={{0,192},{1,193},{2,194},{3,195},{4,196},{5,197},{6,198},{7,199},{8... | collective-permute-start | bytes 393224 | tf_op jit(solution)/shard_map/ppermute | solution.py:31
  25.8 1.0 copy-start
  26.8 0.9 copy-start.3
  27.8 0.7 copy-start.4
  29.5 21.4 %collective-permute-start.13 = (bf16[528,256]{1,0:T(8,128)(2,1)S(1)}, bf16[528,256]{1,0:T(8,128)(2,1)S(1)}, u32[]{:S(2)}, u32[]{:S(2)}) collective-permute-start(bf16[528,256]{1,0:T(8,128)(2,1)S(1)} %project.3.n0), channel_id=1, source_target_pairs={{0,16},{1,17},{2,18},{3,19},{4,20},{5,21},{6,22},{7,23},{8,24},{9,... | collective-permute-start | bytes 811016 | tf_op jit(solution)/shard_map/ppermute | solution.py:31
  31.5 10.2 %collective-permute-start.6 = (bf16[64,1024]{1,0:T(8,128)(2,1)S(1)}, bf16[64,1024]{1,0:T(8,128)(2,1)S(1)}, u32[]{:S(2)}, u32[]{:S(2)}) collective-permute-start(bf16[64,1024]{1,0:T(8,128)(2,1)S(1)} %pad_maximum_fusion.1.q0), channel_id=1, source_target_pairs={{0,128},{1,129},{2,130},{3,131},{4,132},{5,133},{6,134},{7,135},{8... | collective-permute-start | bytes 393224 | tf_op jit(solution)/shard_map/ppermute | solution.py:31
  33.8 14.7 %collective-permute-start.1 = (bf16[128,1024]{1,0:T(8,128)(2,1)S(1)}, bf16[128,1024]{1,0:T(8,128)(2,1)S(1)}, u32[]{:S(2)}, u32[]{:S(2)}) collective-permute-start(bf16[128,1024]{1,0:T(8,128)(2,1)S(1)} %collective-permute-done.e0), channel_id=1, source_target_pairs={{0,6},{1,7},{2,0},{3,1},{4,2},{5,3},{6,4},{7,5},{8,14},{9,15},{10,... | collective-permute-start | bytes 786440 | tf_op jit(solution)/shard_map/ppermute | solution.py:31
  36.4 12.0 %collective-permute-start.2 = (bf16[128,1024]{1,0:T(8,128)(2,1)S(1)}, bf16[128,1024]{1,0:T(8,128)(2,1)S(1)}, u32[]{:S(2)}, u32[]{:S(2)}) collective-permute-start(bf16[128,1024]{1,0:T(8,128)(2,1)S(1)} %collective-permute-done.e0), channel_id=1, source_target_pairs={{0,4},{1,5},{2,6},{3,7},{4,0},{5,1},{6,2},{7,3},{8,12},{9,13},{10,... | collective-permute-start | bytes 786440 | tf_op jit(solution)/shard_map/ppermute | solution.py:31
  37.3 13.5 %collective-permute-start.3 = (bf16[128,1024]{1,0:T(8,128)(2,1)S(1)}, bf16[128,1024]{1,0:T(8,128)(2,1)S(1)}, u32[]{:S(2)}, u32[]{:S(2)}) collective-permute-start(bf16[128,1024]{1,0:T(8,128)(2,1)S(1)} %collective-permute-done.e0), channel_id=1, source_target_pairs={{0,2},{1,3},{2,4},{3,5},{4,6},{5,7},{6,0},{7,1},{8,10},{9,11},{10,... | collective-permute-start | bytes 786440 | tf_op jit(solution)/shard_map/ppermute | solution.py:31
  41.7 6.8 %collective-permute-start.7 = (bf16[64,1024]{1,0:T(8,128)(2,1)S(1)}, bf16[64,1024]{1,0:T(8,128)(2,1)S(1)}, u32[]{:S(2)}, u32[]{:S(2)}) collective-permute-start(bf16[64,1024]{1,0:T(8,128)(2,1)S(1)} %pad_maximum_fusion.1.q0), channel_id=1, source_target_pairs={{0,64},{1,65},{2,66},{3,67},{4,68},{5,69},{6,70},{7,71},{8,72},{9,... | collective-permute-start | bytes 393224 | tf_op jit(solution)/shard_map/ppermute | solution.py:31
  48.4 4.3 %collective-permute-start.12 = (bf16[528,256]{1,0:T(8,128)(2,1)S(1)}, bf16[528,256]{1,0:T(8,128)(2,1)S(1)}, u32[]{:S(2)}, u32[]{:S(2)}) collective-permute-start(bf16[528,256]{1,0:T(8,128)(2,1)S(1)} %project.3.n0), channel_id=1, source_target_pairs={{0,8},{1,9},{2,10},{3,11},{4,12},{5,13},{6,14},{7,15},{8,0},{9,1},... | collective-permute-start | bytes 811016 | tf_op jit(solution)/shard_map/ppermute | solution.py:31
  50.8 1.9 %collective-permute-start.14 = (bf16[528,256]{1,0:T(8,128)(2,1)S(1)}, bf16[528,256]{1,0:T(8,128)(2,1)S(1)}, u32[]{:S(2)}, u32[]{:S(2)}) collective-permute-start(bf16[528,256]{1,0:T(8,128)(2,1)S(1)} %collective-permute-done.13.n2), channel_id=1, source_target_pairs={{0,8},{1,9},{2,10},{3,11},{4,12},{5,13},{6,14},{7,15},{8,0},{9,1},... | collective-permute-start | bytes 811016 | tf_op jit(solution)/shard_map/ppermute | solution.py:31
  51.8 9.0 %collective-permute-start.8 = (bf16[528,256]{1,0:T(8,128)(2,1)S(1)}, bf16[528,256]{1,0:T(8,128)(2,1)S(1)}, u32[]{:S(2)}, u32[]{:S(2)}) collective-permute-start(bf16[528,256]{1,0:T(8,128)(2,1)S(1)} %project.2.n0), channel_id=1, source_target_pairs={{0,16},{1,17},{2,18},{3,19},{4,20},{5,21},{6,22},{7,23},{8,24},{9,... | collective-permute-start | bytes 811016 | tf_op jit(solution)/shard_map/ppermute | solution.py:31
  52.3 8.5 %collective-permute-start.15 = (bf16[528,256]{1,0:T(8,128)(2,1)S(1)}, bf16[528,256]{1,0:T(8,128)(2,1)S(1)}, u32[]{:S(2)}, u32[]{:S(2)}) collective-permute-start(bf16[528,256]{1,0:T(8,128)(2,1)S(1)} %project.2.n0), channel_id=1, source_target_pairs={{0,8},{1,9},{2,10},{3,11},{4,12},{5,13},{6,14},{7,15},{8,0},{9,1},... | collective-permute-start | bytes 811016 | tf_op jit(solution)/shard_map/ppermute | solution.py:31
  60.8 1.5 %collective-permute-start.16 = (bf16[528,256]{1,0:T(8,128)(2,1)S(1)}, bf16[528,256]{1,0:T(8,128)(2,1)S(1)}, u32[]{:S(2)}, u32[]{:S(2)}) collective-permute-start(bf16[528,256]{1,0:T(8,128)(2,1)S(1)} %collective-permute-done.8.n2), channel_id=1, source_target_pairs={{0,8},{1,9},{2,10},{3,11},{4,12},{5,13},{6,14},{7,15},{8,0},{9,1},... | collective-permute-start | bytes 811016 | tf_op jit(solution)/shard_map/ppermute | solution.py:31
  64.8 11.7 %collective-permute-start.19 = (bf16[64,1152]{1,0:T(8,128)(2,1)S(1)}, bf16[64,1152]{1,0:T(8,128)(2,1)S(1)}, u32[]{:S(2)}, u32[]{:S(2)}) collective-permute-start(bf16[64,1152]{1,0:T(8,128)(2,1)S(1)} %attend_far.7), channel_id=1, source_target_pairs={{0,192},{1,193},{2,194},{3,195},{4,196},{5,197},{6,198},{7,199},{8... | collective-permute-start | bytes 442376 | tf_op jit(solution)/shard_map/ppermute | solution.py:31
  68.7 7.8 %collective-permute-start.18 = (bf16[64,1152]{1,0:T(8,128)(2,1)S(1)}, bf16[64,1152]{1,0:T(8,128)(2,1)S(1)}, u32[]{:S(2)}, u32[]{:S(2)}) collective-permute-start(bf16[64,1152]{1,0:T(8,128)(2,1)S(1)} %attend_far.6), channel_id=1, source_target_pairs={{0,128},{1,129},{2,130},{3,131},{4,132},{5,133},{6,134},{7,135},{8... | collective-permute-start | bytes 442376 | tf_op jit(solution)/shard_map/ppermute | solution.py:31
  71.2 23.3 %copy-start.2 = (bf16[4,1024,256]{2,1,0:T(8,128)(2,1)S(1)}, bf16[4,1024,256]{2,1,0:T(8,128)(2,1)}, u32[]{:S(2)}) copy-start(bf16[4,1024,256]{2,1,0:T(8,128)(2,1)} %all-gather.2.cloned.1.call-done.weights) | copy-start | bytes 6291460
  71.2 7.0 %collective-permute-start.17 = (bf16[64,1152]{1,0:T(8,128)(2,1)S(1)}, bf16[64,1152]{1,0:T(8,128)(2,1)S(1)}, u32[]{:S(2)}, u32[]{:S(2)}) collective-permute-start(bf16[64,1152]{1,0:T(8,128)(2,1)S(1)} %attend_far.5), channel_id=1, source_target_pairs={{0,64},{1,65},{2,66},{3,67},{4,68},{5,69},{6,70},{7,71},{8,72},{9,... | collective-permute-start | bytes 442376 | tf_op jit(solution)/shard_map/ppermute | solution.py:31
  78.8 44.1 %copy-start.5 = (bf16[128,256]{1,0:T(8,128)(2,1)S(1)}, bf16[128,256]{1,0:T(8,128)(2,1)}, u32[]{:S(2)}) copy-start(bf16[128,256]{1,0:T(8,128)(2,1)} %param.11) | copy-start | bytes 196612
  78.8 8.6 %collective-permute-start.20 = (bf16[64,1152]{1,0:T(8,128)(2,1)S(1)}, bf16[64,1152]{1,0:T(8,128)(2,1)S(1)}, u32[]{:S(2)}, u32[]{:S(2)}) collective-permute-start(bf16[64,1152]{1,0:T(8,128)(2,1)S(1)} %fold.2.refs_0_), channel_id=1, source_target_pairs={{0,32},{1,33},{2,34},{3,35},{4,36},{5,37},{6,38},{7,39},{8,40},{9,... | collective-permute-start | bytes 442376 | tf_op jit(solution)/shard_map/ppermute | solution.py:31
  87.8 5.1 %collective-permute-start.21 = (bf16[64,1024]{1,0:T(8,128)(2,1)S(1)}, bf16[64,1024]{1,0:T(8,128)(2,1)S(1)}, u32[]{:S(2)}, u32[]{:S(2)}) collective-permute-start(bf16[64,1024]{1,0:T(8,128)(2,1)S(1)} %fold.3.own), channel_id=1, source_target_pairs={{0,16},{1,17},{2,18},{3,19},{4,20},{5,21},{6,22},{7,23},{8,24},{9,... | collective-permute-start | bytes 393224 | tf_op jit(solution)/shard_map/ppermute | solution.py:31
  92.9 1.6 %collective-permute-start.22 = (bf16[128,1024]{1,0:T(8,128)(2,1)S(1)}, bf16[128,1024]{1,0:T(8,128)(2,1)S(1)}, u32[]{:S(2)}, u32[]{:S(2)}) collective-permute-start(bf16[128,1024]{1,0:T(8,128)(2,1)S(1)} %pad_maximum_fusion), channel_id=1, source_target_pairs={{0,8},{1,9},{2,10},{3,11},{4,12},{5,13},{6,14},{7,15},{8,0},{9,1},... | collective-permute-start | bytes 786440 | tf_op jit(solution)/shard_map/ppermute | solution.py:31
  95.8 9.3 %collective-permute-start.23 = (bf16[256,256]{1,0:T(8,128)(2,1)S(1)}, bf16[256,256]{1,0:T(8,128)(2,1)S(1)}, u32[]{:S(2)}, u32[]{:S(2)}) collective-permute-start(bf16[256,256]{1,0:T(8,128)(2,1)S(1)} %get-tuple-element.35), channel_id=1, source_target_pairs={{0,0},{1,1},{2,2},{3,3},{4,4},{5,5},{6,6},{7,7},{8,8},{9,9},{10,10... | collective-permute-start | bytes 393224 | tf_op jit(solution)/shard_map/ppermute | solution.py:31
  97.7 7.4 %collective-permute-start.24 = (bf16[256,256]{1,0:T(8,128)(2,1)S(1)}, bf16[256,256]{1,0:T(8,128)(2,1)S(1)}, u32[]{:S(2)}, u32[]{:S(2)}) collective-permute-start(bf16[256,256]{1,0:T(8,128)(2,1)S(1)} %get-tuple-element.36), channel_id=1, source_target_pairs={{0,64},{1,65},{2,66},{3,67},{4,68},{5,69},{6,70},{7,71},{8,72},{9,... | collective-permute-start | bytes 393224 | tf_op jit(solution)/shard_map/ppermute | solution.py:31
  100.9 10.1 %collective-permute-start.25 = (bf16[256,256]{1,0:T(8,128)(2,1)S(1)}, bf16[256,256]{1,0:T(8,128)(2,1)S(1)}, u32[]{:S(2)}, u32[]{:S(2)}) collective-permute-start(bf16[256,256]{1,0:T(8,128)(2,1)S(1)} %get-tuple-element.37), channel_id=1, source_target_pairs={{0,128},{1,129},{2,130},{3,131},{4,132},{5,133},{6,134},{7,135},{8... | collective-permute-start | bytes 393224 | tf_op jit(solution)/shard_map/ppermute | solution.py:31
  101.8 12.2 %collective-permute-start.26 = (bf16[256,256]{1,0:T(8,128)(2,1)S(1)}, bf16[256,256]{1,0:T(8,128)(2,1)S(1)}, u32[]{:S(2)}, u32[]{:S(2)}) collective-permute-start(bf16[256,256]{1,0:T(8,128)(2,1)S(1)} %get-tuple-element.38), channel_id=1, source_target_pairs={{0,192},{1,193},{2,194},{3,195},{4,196},{5,197},{6,198},{7,199},{8... | collective-permute-start | bytes 393224 | tf_op jit(solution)/shard_map/ppermute | solution.py:31
  114.6 8.3 %collective-permute-start.27 = (bf16[128,256]{1,0:T(8,128)(2,1)S(1)}, bf16[128,256]{1,0:T(8,128)(2,1)S(1)}, u32[]{:S(2)}, u32[]{:S(2)}) collective-permute-start(bf16[128,256]{1,0:T(8,128)(2,1)S(1)} %get-tuple-element.40), channel_id=1, source_target_pairs={{0,1},{1,0},{2,3},{3,2},{4,5},{5,4},{6,7},{7,6},{8,9},{9,8},{10,11... | collective-permute-start | bytes 196616 | tf_op jit(solution)/shard_map/ppermute | solution.py:31
Sparse Core Ops, SparseCore 0:
  9.2 39.1 all-gather.1

commit v2 on v1

--- a/solution.py
+++ b/solution.py
@@ -190,8 +190,9 @@
             emit(i, sums, packed)
 
 
-def near_kernel(q0, q1, q2, q3, n0, n1, n2, n3, q_all, sums_all, stats_all, valued):
-    queries = (q0, q1, q2, q3)
+def near_kernel(*refs):
+    queries, parts = refs[:4], refs[4:-4]
+    q_all, sums_all, stats_all, valued = refs[-4:]
     for i, q in enumerate(queries):
         q_all[i] = q[...]
 
@@ -200,7 +201,7 @@
             sums_all[i, :, h * HD : (h + 1) * HD] = value
         stats_all[i] = packed
 
-    attend_kernel(queries, (n0, n1, n2, n3), (None,) * 4, valued, emit)
+    attend_kernel(queries, parts, (None,) * 4, valued, emit)
 
 
 def attend_near(queries, kv):
@@ -212,16 +213,17 @@
             jax.ShapeDtypeStruct((4, count, GROUP * HD), f32),
             jax.ShapeDtypeStruct((4, count, HD), f32),
         ),
-        in_specs=vmem(8),
+        in_specs=vmem(4 + len(kv)),
         out_specs=tuple(vmem(3)),
-        scratch_shapes=[pltpu.VMEM((2048, 2 * HD), bf16)],
+        scratch_shapes=[pltpu.VMEM((512 * len(kv), 2 * HD), bf16)],
         compiler_params=PARAMS,
         cost_estimate=cost(1024, 1024),
         name="attend_near",
     )(*queries, *kv)
 
 
-def far_kernel(k, place_ref, q_all, n0, n1, n2, n3, sums_all, stats_all, out, valued):
+def far_kernel(k, place_ref, q_all, sums_all, stats_all, *rest):
+    parts, out, valued = rest[:-2], rest[-2], rest[-1]
     count = q_all.shape[1]
     at = lax.rem(place_ref[1] + k, 4)
 
@@ -231,7 +233,7 @@
         put_stats(out, packed)
 
     carry = (sums_all.at[at], stats_all[at])
-    attend_kernel((q_all.at[at],), (n0, n1, n2, n3), (carry,), valued, emit)
+    attend_kernel((q_all.at[at],), parts, (carry,), valued, emit)
 
 
 def attend_far(k, place, carries, kv):
@@ -240,13 +242,13 @@
     return pl.pallas_call(
         functools.partial(far_kernel, k),
         out_shape=jax.ShapeDtypeStruct((count, GROUP * HD + HD), bf16),
-        in_specs=[SMEM] + vmem(7),
+        in_specs=[SMEM] + vmem(3 + len(kv)),
         out_specs=vmem(1)[0],
-        scratch_shapes=[pltpu.VMEM((2048, 2 * HD), bf16)],
-        compiler_params=PARAMS,
-        cost_estimate=cost(4 * 512 * 2048 * 256, 2 << 20, 512 * 2048),
+        scratch_shapes=[pltpu.VMEM((512 * len(kv), 2 * HD), bf16)],
+        compiler_params=PARAMS,
+        cost_estimate=cost(4 * 512 * 1024 * 256, 2 << 20, 512 * 1024),
         name="attend_far",
-    )(place, q_all, *kv, sums_all, stats_all)
+    )(place, q_all, sums_all, stats_all, *kv)
 
 
 def fold_kernel(last, *refs):
@@ -285,10 +287,9 @@
     )(*parts)
 
 
-def output_kernel(place_ref, own, beside, other, weights, o0, o1, o2, o3, rows):
+def output_kernel(place_ref, r0, r1, r2, r3, weights, o0, o1, o2, o3, rows):
     y, z, c = place_ref[0], place_ref[3], place_ref[4]
-    blocks = [own.at[:32], own.at[32:], beside.at[:32], beside.at[32:]]
-    blocks += [other.at[i * 32 : (i + 1) * 32] for i in range(4)]
+    blocks = [r.at[i : i + 32] for r in (r0, r1, r2, r3) for i in (0, 32)]
     for i, block in enumerate(blocks):
         core = (1 - c) if i >= 4 else c
         at = (jnp.bitwise_xor(z, Z_ORDER[i % 4]) * 2 + core) * 32
@@ -298,17 +299,17 @@
         out[...] = jnp.dot(rows[...], weight, preferred_element_type=f32).astype(bf16)
 
 
-def output_terms(place, own, beside, other, weights):
+def output_terms(place, rows, weights):
     return pl.pallas_call(
         output_kernel,
         out_shape=tuple([jax.ShapeDtypeStruct((256, 256), bf16)] * 4),
-        in_specs=[SMEM] + vmem(4),
+        in_specs=[SMEM] + vmem(5),
         out_specs=tuple(vmem(4)),
         scratch_shapes=[pltpu.VMEM((256, GROUP * HD), bf16)],
         compiler_params=PARAMS,
         cost_estimate=cost(2 * 256 * 1024 * 1024, 3 << 20),
         name="output",
-    )(place, own, beside, other, weights)
+    )(place, *rows, weights)
 
 
 def sum_kernel(place_ref, t0, t1, t2, t3, mine, other):
@@ -350,13 +351,14 @@
 
     kv_near = project(False, place, span_lens, near, weight)
     beside = swap_z(kv_near, 1)
-    kv_near = kv_near, other_core(kv_near), beside, other_core(beside)
-    carries = attend_near(all_q, kv_near)
+    here = [kv_near, other_core(kv_near), beside, other_core(beside)]
     far = lax.optimization_barrier(far + all_q)[:4]
     kv_far = project(True, place, span_lens, far, weight)
     beside = swap_z(kv_far, 1)
+    here += [kv_far, other_core(kv_far)]
+    carries = attend_near(all_q, here)
     beside, carries, weights = lax.optimization_barrier((beside, carries, weights))
-    kv_far = kv_far, other_core(kv_far), beside, other_core(beside)
+    kv_far = beside, other_core(beside)
 
     parts = [None] * 4
     for k in (2, 1, 3, 0):
@@ -366,8 +368,8 @@
     joint = fold(64, parts)
     own = fold(64, (joint, swap_z(joint, 2)), last=True)
     beside = swap_z(own, 1)
-    other = other_core(jnp.concatenate([own, beside], axis=0))
-    terms = output_terms(place, own, beside, other, weights)
+    rows = [own, beside, other_core(own), other_core(beside)]
+    terms = output_terms(place, rows, weights)
     terms = [
         move(term, lambda y, z, c, x, h, j=j: (y + j, z, c, x + y, h))
         for j, term in enumerate(terms)

time: 131 us -> 130 us (level)
  waiting for transfers between devices: 48.5 us -> 42.4 us
  starting transfers between devices: 44.1 us -> 49 us
    ppermute x28 -> x29, waiting for transfers between devices: 47.8 us -> 41.6 us  [move(): return lax.ppermute(value, AXES, pairs)]
    ppermute x28 -> x29, starting transfers between devices: 44.1 us -> 49 us  [move(): return lax.ppermute(value, AXES, pairs)]
    pallas_call x4, Pallas kernels: 9.78 us -> 7.13 us  [attend_far(): pl.pallas_call(functools.partial(far_kernel, k), out_shape=jax.ShapeDtype...]
    pallas_call x1, Pallas kernels: 5.39 us -> 7.82 us  [attend_near(): pl.pallas_call(near_kernel, out_shape=(jax.ShapeDtypeStruct((4, count, GR...]
  transfers between devices with their start and end apart: 29 -> 30, of which waited for: 15 -> 13; matrix products, arithmetic and copies ran while one was open for 1% -> 1% of each run, Pallas kernels for 11% -> 12%
where the time goes in v2:
time: 130 us; the launch traced here: 129 us
  starting transfers between devices  49 us (38%)
  waiting for transfers between devices  42.4 us (33%)
  Pallas kernels  19.8 us (15%)
  between operations  13.6 us (10%)
  local copies, waits for them, and re-layouts  2.74 us (2%)
  other arithmetic  1.51 us (1%)
    ppermute x29, starting transfers between devices, move(): return lax.ppermute(value, AXES, pairs)  49 us
    ppermute x29, waiting for transfers between devices, move(): return lax.ppermute(value, AXES, pairs)  41.6 us
    pallas_call x1, Pallas kernels, attend_near(): pl.pallas_call(near_kernel, out_shape=(jax.ShapeDtypeStruct((4, count, GR...  7.82 us
    pallas_call x4, Pallas kernels, attend_far(): pl.pallas_call(functools.partial(far_kernel, k), out_shape=jax.ShapeDtype...  7.13 us
    unnamed x12, local copies, waits for them, and re-layouts  2.66 us
  transfers between devices with their start and end apart: 30, of which 13 were waited for; matrix products, arithmetic and copies ran while one was open for 1% of the time, Pallas kernels for 12%

profile of v2, /device:TPU:8, one launch (start us, length us, event | category | flops | bytes accessed | tf_op | source)
XLA Modules:
  0.0 129.0 jit_solution(7087067453528153139)
XLA Ops:
  6.5 0.7 all-gather.2.cloned.1.call-update
  7.3 3.4 %collective-permute-start.4 = (bf16[32,1024]{1,0:T(8,128)(2,1)}, bf16[32,1024]{1,0:T(8,128)(2,1)S(1)}, u32[]{:S(2)}, u32[]{:S(2)}) collective-permute-start(bf16[32,1024]{1,0:T(8,128)(2,1)} %bitcast.9), channel_id=1, source_target_pairs={{0,32},{1,33},{2,34},{3,35},{4,36},{5,37},{6,38},{7,39},{8,40},{9,... | collective-permute-start | bytes 196616 | tf_op jit(solution)/shard_map/ppermute | solution.py:31
  10.6 5.4 %collective-permute-start = (bf16[128,1024]{1,0:T(8,128)(2,1)}, bf16[128,1024]{1,0:T(8,128)(2,1)S(1)}, u32[]{:S(2)}, u32[]{:S(2)}) collective-permute-start(bf16[128,1024]{1,0:T(8,128)(2,1)} %e0.1), channel_id=1, source_target_pairs={{0,1},{1,0},{2,3},{3,2},{4,5},{5,4},{6,7},{7,6},{8,9},{9,8},{10,11... | collective-permute-start | bytes 786440 | tf_op jit(solution)/shard_map/ppermute | solution.py:31
  16.0 3.0 %collective-permute-start.10 = (bf16[128,1024]{1,0:T(8,128)(2,1)}, bf16[128,1024]{1,0:T(8,128)(2,1)S(1)}, u32[]{:S(2)}, u32[]{:S(2)}) collective-permute-start(bf16[128,1024]{1,0:T(8,128)(2,1)} %e0.1), channel_id=1, source_target_pairs={{0,4},{1,5},{2,6},{3,7},{4,0},{5,1},{6,2},{7,3},{8,12},{9,13},{10,... | collective-permute-start | bytes 786440 | tf_op jit(solution)/shard_map/ppermute | solution.py:31
  19.0 0.6 collective-permute-start.11
  19.6 2.6 %collective-permute-start.9 = (bf16[128,1024]{1,0:T(8,128)(2,1)}, bf16[128,1024]{1,0:T(8,128)(2,1)S(1)}, u32[]{:S(2)}, u32[]{:S(2)}) collective-permute-start(bf16[128,1024]{1,0:T(8,128)(2,1)} %e0.1), channel_id=1, source_target_pairs={{0,6},{1,7},{2,0},{3,1},{4,2},{5,3},{6,4},{7,5},{8,14},{9,15},{10,... | collective-permute-start | bytes 786440 | tf_op jit(solution)/shard_map/ppermute | solution.py:31
  22.3 0.8 pad_maximum_fusion.refs_0_
  23.1 0.5 collective-permute-start.5
  23.7 4.0 %collective-permute-done.e0 = bf16[128,1024]{1,0:T(8,128)(2,1)S(1)} collective-permute-done((bf16[128,1024]{1,0:T(8,128)(2,1)}, bf16[128,1024]{1,0:T(8,128)(2,1)S(1)}, u32[]{:S(2)}, u32[]{:S(2)}) %collective-permute-start) | collective-permute-done | bytes 262176 | tf_op jit(solution)/shard_map/ppermute | solution.py:31
  27.6 2.3 %collective-permute-start.6 = (bf16[64,1024]{1,0:T(8,128)(2,1)S(1)}, bf16[64,1024]{1,0:T(8,128)(2,1)S(1)}, u32[]{:S(2)}, u32[]{:S(2)}) collective-permute-start(bf16[64,1024]{1,0:T(8,128)(2,1)S(1)} %pad_maximum_fusion.refs_0_), channel_id=1, source_target_pairs={{0,128},{1,129},{2,130},{3,131},{4,132},{5,133},{6,134},{7,135},{8... | collective-permute-start | bytes 393224 | tf_op jit(solution)/shard_map/ppermute | solution.py:31
  29.9 2.8 %collective-permute-start.1 = (bf16[128,1024]{1,0:T(8,128)(2,1)S(1)}, bf16[128,1024]{1,0:T(8,128)(2,1)S(1)}, u32[]{:S(2)}, u32[]{:S(2)}) collective-permute-start(bf16[128,1024]{1,0:T(8,128)(2,1)S(1)} %collective-permute-done.e0), channel_id=1, source_target_pairs={{0,6},{1,7},{2,0},{3,1},{4,2},{5,3},{6,4},{7,5},{8,14},{9,15},{10,... | collective-permute-start | bytes 786440 | tf_op jit(solution)/shard_map/ppermute | solution.py:31
  32.7 0.8 collective-permute-start.2
  33.5 0.9 collective-permute-start.3
  34.5 1.0 copy-done
  35.5 0.9 copy-done.3
  36.5 0.7 copy-done.4
  37.1 1.0 project.3.refs_4_
  38.1 3.4 %collective-permute-start.13 = (bf16[528,256]{1,0:T(8,128)(2,1)S(1)}, bf16[528,256]{1,0:T(8,128)(2,1)S(1)}, u32[]{:S(2)}, u32[]{:S(2)}) collective-permute-start(bf16[528,256]{1,0:T(8,128)(2,1)S(1)} %project.3.refs_4_), channel_id=1, source_target_pairs={{0,16},{1,17},{2,18},{3,19},{4,20},{5,21},{6,22},{7,23},{8,24},{9,... | collective-permute-start | bytes 811016 | tf_op jit(solution)/shard_map/ppermute | solution.py:31
  41.5 7.0 %collective-permute-done.7.refs_3_ = bf16[64,1024]{1,0:T(8,128)(2,1)S(1)} collective-permute-done((bf16[64,1024]{1,0:T(8,128)(2,1)S(1)}, bf16[64,1024]{1,0:T(8,128)(2,1)S(1)}, u32[]{:S(2)}, u32[]{:S(2)}) %collective-permute-start.7) | collective-permute-done | bytes 131104 | tf_op jit(solution)/shard_map/ppermute | solution.py:31
  48.5 1.0 project.2.refs_8_
  49.5 0.6 collective-permute-start.15
  50.2 1.1 collective-permute-start.8
  51.6 7.8 %attend_near.1 = (bf16[4,64,1024]{2,1,0:T(8,128)(2,1)S(1)}, f32[4,64,1024]{2,1,0:T(8,128)S(1)}, f32[4,64,128]{2,1,0:T(8,128)S(1)}) custom-call(bf16[64,1024]{1,0:T(8,128)(2,1)S(1)} %pad_maximum_fusion.refs_0_, bf16[64,1024]{1,0:T(8,128)(2,1)S(1)} %collective-permute-done.5.refs_1_, bf16[64,1024]{1,0:T(8,128)(2,1)S(1)} %collective-permute-done.6.refs_2_, ...), custom_call_target="tpu_custom_call" | custom-call | flops 1024 | bytes 1024 | tf_op jit(solution)/shard_map/attend_near/pallas_call | solution.py:209
  60.0 1.2 collective-permute-done.16.rest_1_
  61.1 1.8 %attend_far.7 = bf16[64,1152]{1,0:T(8,128)(2,1)S(1)} custom-call(s32[5]{0:T(128)S(1)} %stack.23.place_ref, bf16[4,64,1024]{2,1,0:T(8,128)(2,1)S(1)} %get-tuple-element.30.q_all, f32[4,64,1024]{2,1,0:T(8,128)S(1)} %get-tuple-element.31.sums_all, f32[4,64,128]{2,1,0:T(8,128)S(1)} %get-tuple-element.32.stats_all, ...), custom_call_target="tpu_custom_call" | custom-call | flops 536870912 | bytes 2097152 | tf_op jit(solution)/shard_map/attend_far/pallas_call | solution.py:242
  62.9 2.9 %collective-permute-start.19 = (bf16[64,1152]{1,0:T(8,128)(2,1)S(1)}, bf16[64,1152]{1,0:T(8,128)(2,1)S(1)}, u32[]{:S(2)}, u32[]{:S(2)}) collective-permute-start(bf16[64,1152]{1,0:T(8,128)(2,1)S(1)} %attend_far.7), channel_id=1, source_target_pairs={{0,192},{1,193},{2,194},{3,195},{4,196},{5,197},{6,198},{7,199},{8... | collective-permute-start | bytes 442376 | tf_op jit(solution)/shard_map/ppermute | solution.py:31
  65.8 1.8 %attend_far.6 = bf16[64,1152]{1,0:T(8,128)(2,1)S(1)} custom-call(s32[5]{0:T(128)S(1)} %stack.23.place_ref, bf16[4,64,1024]{2,1,0:T(8,128)(2,1)S(1)} %get-tuple-element.30.q_all, f32[4,64,1024]{2,1,0:T(8,128)S(1)} %get-tuple-element.31.sums_all, f32[4,64,128]{2,1,0:T(8,128)S(1)} %get-tuple-element.32.stats_all, ...), custom_call_target="tpu_custom_call" | custom-call | flops 536870912 | bytes 2097152 | tf_op jit(solution)/shard_map/attend_far/pallas_call | solution.py:242
  68.0 1.8 %attend_far.5 = bf16[64,1152]{1,0:T(8,128)(2,1)S(1)} custom-call(s32[5]{0:T(128)S(1)} %stack.23.place_ref, bf16[4,64,1024]{2,1,0:T(8,128)(2,1)S(1)} %get-tuple-element.30.q_all, f32[4,64,1024]{2,1,0:T(8,128)S(1)} %get-tuple-element.31.sums_all, f32[4,64,128]{2,1,0:T(8,128)S(1)} %get-tuple-element.32.stats_all, ...), custom_call_target="tpu_custom_call" | custom-call | flops 536870912 | bytes 2097152 | tf_op jit(solution)/shard_map/attend_far/pallas_call | solution.py:242
  69.8 2.0 %collective-permute-start.17 = (bf16[64,1152]{1,0:T(8,128)(2,1)S(1)}, bf16[64,1152]{1,0:T(8,128)(2,1)S(1)}, u32[]{:S(2)}, u32[]{:S(2)}) collective-permute-start(bf16[64,1152]{1,0:T(8,128)(2,1)S(1)} %attend_far.5), channel_id=1, source_target_pairs={{0,64},{1,65},{2,66},{3,67},{4,68},{5,69},{6,70},{7,71},{8,72},{9,... | collective-permute-start | bytes 442376 | tf_op jit(solution)/shard_map/ppermute | solution.py:31
  71.7 1.8 %attend_far.4.refs_0_ = bf16[64,1152]{1,0:T(8,128)(2,1)S(1)} custom-call(s32[5]{0:T(128)S(1)} %stack.23.place_ref, bf16[4,64,1024]{2,1,0:T(8,128)(2,1)S(1)} %get-tuple-element.30.q_all, f32[4,64,1024]{2,1,0:T(8,128)S(1)} %get-tuple-element.31.sums_all, f32[4,64,128]{2,1,0:T(8,128)S(1)} %get-tuple-element.32.stats_all, ...), custom_call_target="tpu_custom_call" | custom-call | flops 536870912 | bytes 2097152 | tf_op jit(solution)/shard_map/attend_far/pallas_call | solution.py:242
  73.5 1.7 %collective-permute-done.18.refs_2_ = bf16[64,1152]{1,0:T(8,128)(2,1)S(1)} collective-permute-done((bf16[64,1152]{1,0:T(8,128)(2,1)S(1)}, bf16[64,1152]{1,0:T(8,128)(2,1)S(1)}, u32[]{:S(2)}, u32[]{:S(2)}) %collective-permute-start.18) | collective-permute-done | bytes 147488 | tf_op jit(solution)/shard_map/ppermute | solution.py:31
  75.3 0.9 collective-permute-done.17.refs_1_
  76.2 0.5 fold.2.refs_0_
  76.7 0.6 collective-permute-start.20
  77.3 8.9 %collective-permute-done.20.refs_1_ = bf16[64,1152]{1,0:T(8,128)(2,1)S(1)} collective-permute-done((bf16[64,1152]{1,0:T(8,128)(2,1)S(1)}, bf16[64,1152]{1,0:T(8,128)(2,1)S(1)}, u32[]{:S(2)}, u32[]{:S(2)}) %collective-permute-start.20) | collective-permute-done | bytes 147488 | tf_op jit(solution)/shard_map/ppermute | solution.py:31
  86.8 5.0 %collective-permute-done.21.r1 = bf16[64,1024]{1,0:T(8,128)(2,1)S(1)} collective-permute-done((bf16[64,1024]{1,0:T(8,128)(2,1)S(1)}, bf16[64,1024]{1,0:T(8,128)(2,1)S(1)}, u32[]{:S(2)}, u32[]{:S(2)}) %collective-permute-start.21) | collective-permute-done | bytes 131104 | tf_op jit(solution)/shard_map/ppermute | solution.py:31
  91.9 1.3 %collective-permute-done.23.r3 = bf16[64,1024]{1,0:T(8,128)(2,1)S(1)} collective-permute-done((bf16[64,1024]{1,0:T(8,128)(2,1)S(1)}, bf16[64,1024]{1,0:T(8,128)(2,1)S(1)}, u32[]{:S(2)}, u32[]{:S(2)}) %collective-permute-start.23) | collective-permute-done | bytes 131104 | tf_op jit(solution)/shard_map/ppermute | solution.py:31
  93.2 1.3 output.1
  94.5 3.2 %collective-permute-start.24 = (bf16[256,256]{1,0:T(8,128)(2,1)S(1)}, bf16[256,256]{1,0:T(8,128)(2,1)S(1)}, u32[]{:S(2)}, u32[]{:S(2)}) collective-permute-start(bf16[256,256]{1,0:T(8,128)(2,1)S(1)} %get-tuple-element.35), channel_id=1, source_target_pairs={{0,0},{1,1},{2,2},{3,3},{4,4},{5,5},{6,6},{7,7},{8,8},{9,9},{10,10... | collective-permute-start | bytes 393224 | tf_op jit(solution)/shard_map/ppermute | solution.py:31
  97.7 3.3 %collective-permute-start.25 = (bf16[256,256]{1,0:T(8,128)(2,1)S(1)}, bf16[256,256]{1,0:T(8,128)(2,1)S(1)}, u32[]{:S(2)}, u32[]{:S(2)}) collective-permute-start(bf16[256,256]{1,0:T(8,128)(2,1)S(1)} %get-tuple-element.36), channel_id=1, source_target_pairs={{0,64},{1,65},{2,66},{3,67},{4,68},{5,69},{6,70},{7,71},{8,72},{9,... | collective-permute-start | bytes 393224 | tf_op jit(solution)/shard_map/ppermute | solution.py:31
  101.2 2.4 %collective-permute-start.27 = (bf16[256,256]{1,0:T(8,128)(2,1)S(1)}, bf16[256,256]{1,0:T(8,128)(2,1)S(1)}, u32[]{:S(2)}, u32[]{:S(2)}) collective-permute-start(bf16[256,256]{1,0:T(8,128)(2,1)S(1)} %get-tuple-element.38), channel_id=1, source_target_pairs={{0,192},{1,193},{2,194},{3,195},{4,196},{5,197},{6,198},{7,199},{8... | collective-permute-start | bytes 393224 | tf_op jit(solution)/shard_map/ppermute | solution.py:31
  103.6 1.3 collective-permute-done.25.t1
  104.9 4.9 %collective-permute-done.26.t2 = bf16[256,256]{1,0:T(8,128)(2,1)S(1)} collective-permute-done((bf16[256,256]{1,0:T(8,128)(2,1)S(1)}, bf16[256,256]{1,0:T(8,128)(2,1)S(1)}, u32[]{:S(2)}, u32[]{:S(2)}) %collective-permute-start.26) | collective-permute-done | bytes 131104 | tf_op jit(solution)/shard_map/ppermute | solution.py:31
  109.8 2.8 %collective-permute-done.27.t3 = bf16[256,256]{1,0:T(8,128)(2,1)S(1)} collective-permute-done((bf16[256,256]{1,0:T(8,128)(2,1)S(1)}, bf16[256,256]{1,0:T(8,128)(2,1)S(1)}, u32[]{:S(2)}, u32[]{:S(2)}) %collective-permute-start.27) | collective-permute-done | bytes 131104 | tf_op jit(solution)/shard_map/ppermute | solution.py:31
  112.6 0.6 sum_terms.1
  113.2 6.0 %collective-permute-start.28 = (bf16[128,256]{1,0:T(8,128)(2,1)S(1)}, bf16[128,256]{1,0:T(8,128)(2,1)S(1)}, u32[]{:S(2)}, u32[]{:S(2)}) collective-permute-start(bf16[128,256]{1,0:T(8,128)(2,1)S(1)} %get-tuple-element.40), channel_id=1, source_target_pairs={{0,1},{1,0},{2,3},{3,2},{4,5},{5,4},{6,7},{7,6},{8,9},{9,8},{10,11... | collective-permute-start | bytes 196616 | tf_op jit(solution)/shard_map/ppermute | solution.py:31
  119.3 2.2 %collective-permute-done.28 = bf16[128,256]{1,0:T(8,128)(2,1)S(1)} collective-permute-done((bf16[128,256]{1,0:T(8,128)(2,1)S(1)}, bf16[128,256]{1,0:T(8,128)(2,1)S(1)}, u32[]{:S(2)}, u32[]{:S(2)}) %collective-permute-start.28) | collective-permute-done | bytes 65568 | tf_op jit(solution)/shard_map/ppermute | solution.py:31
  121.5 0.7 add_convert_fusion
  (39 shorter events, 2.3 us)
Async XLA Ops:
  6.5 41.9 %copy-start.1 = (bf16[1024,1,256]{2,0,1:T(8,128)(2,1)S(1)}, bf16[1024,1,256]{2,0,1:T(8,128)(2,1)}, u32[]{:S(2)}) copy-start(bf16[1024,1,256]{2,0,1:T(8,128)(2,1)} %param.8) | copy-start | bytes 1572868
  6.5 52.9 %all-gather.2.cloned.1.call-start = ((), (), s32[]{:S(2)}) async-start(), calls=%async_computation | async-start | bytes 2621440 | tf_op jit(solution)/shard_map/all_gather | solution.py:343
  7.3 15.0 %collective-permute-start.4 = (bf16[32,1024]{1,0:T(8,128)(2,1)}, bf16[32,1024]{1,0:T(8,128)(2,1)S(1)}, u32[]{:S(2)}, u32[]{:S(2)}) collective-permute-start(bf16[32,1024]{1,0:T(8,128)(2,1)} %bitcast.9), channel_id=1, source_target_pairs={{0,32},{1,33},{2,34},{3,35},{4,36},{5,37},{6,38},{7,39},{8,40},{9,... | collective-permute-start | bytes 196616 | tf_op jit(solution)/shard_map/ppermute | solution.py:31
  10.6 17.0 %collective-permute-start = (bf16[128,1024]{1,0:T(8,128)(2,1)}, bf16[128,1024]{1,0:T(8,128)(2,1)S(1)}, u32[]{:S(2)}, u32[]{:S(2)}) collective-permute-start(bf16[128,1024]{1,0:T(8,128)(2,1)} %e0.1), channel_id=1, source_target_pairs={{0,1},{1,0},{2,3},{3,2},{4,5},{5,4},{6,7},{7,6},{8,9},{9,8},{10,11... | collective-permute-start | bytes 786440 | tf_op jit(solution)/shard_map/ppermute | solution.py:31
  16.0 13.9 %collective-permute-start.10 = (bf16[128,1024]{1,0:T(8,128)(2,1)}, bf16[128,1024]{1,0:T(8,128)(2,1)S(1)}, u32[]{:S(2)}, u32[]{:S(2)}) collective-permute-start(bf16[128,1024]{1,0:T(8,128)(2,1)} %e0.1), channel_id=1, source_target_pairs={{0,4},{1,5},{2,6},{3,7},{4,0},{5,1},{6,2},{7,3},{8,12},{9,13},{10,... | collective-permute-start | bytes 786440 | tf_op jit(solution)/shard_map/ppermute | solution.py:31
  19.0 13.6 %collective-permute-start.11 = (bf16[128,1024]{1,0:T(8,128)(2,1)}, bf16[128,1024]{1,0:T(8,128)(2,1)S(1)}, u32[]{:S(2)}, u32[]{:S(2)}) collective-permute-start(bf16[128,1024]{1,0:T(8,128)(2,1)} %e0.1), channel_id=1, source_target_pairs={{0,2},{1,3},{2,4},{3,5},{4,6},{5,7},{6,0},{7,1},{8,10},{9,11},{10,... | collective-permute-start | bytes 786440 | tf_op jit(solution)/shard_map/ppermute | solution.py:31
  19.6 13.9 %collective-permute-start.9 = (bf16[128,1024]{1,0:T(8,128)(2,1)}, bf16[128,1024]{1,0:T(8,128)(2,1)S(1)}, u32[]{:S(2)}, u32[]{:S(2)}) collective-permute-start(bf16[128,1024]{1,0:T(8,128)(2,1)} %e0.1), channel_id=1, source_target_pairs={{0,6},{1,7},{2,0},{3,1},{4,2},{5,3},{6,4},{7,5},{8,14},{9,15},{10,... | collective-permute-start | bytes 786440 | tf_op jit(solution)/shard_map/ppermute | solution.py:31
  23.1 15.0 %collective-permute-start.5 = (bf16[64,1024]{1,0:T(8,128)(2,1)S(1)}, bf16[64,1024]{1,0:T(8,128)(2,1)S(1)}, u32[]{:S(2)}, u32[]{:S(2)}) collective-permute-start(bf16[64,1024]{1,0:T(8,128)(2,1)S(1)} %pad_maximum_fusion.refs_0_), channel_id=1, source_target_pairs={{0,192},{1,193},{2,194},{3,195},{4,196},{5,197},{6,198},{7,199},{8... | collective-permute-start | bytes 393224 | tf_op jit(solution)/shard_map/ppermute | solution.py:31
  27.6 13.9 %collective-permute-start.6 = (bf16[64,1024]{1,0:T(8,128)(2,1)S(1)}, bf16[64,1024]{1,0:T(8,128)(2,1)S(1)}, u32[]{:S(2)}, u32[]{:S(2)}) collective-permute-start(bf16[64,1024]{1,0:T(8,128)(2,1)S(1)} %pad_maximum_fusion.refs_0_), channel_id=1, source_target_pairs={{0,128},{1,129},{2,130},{3,131},{4,132},{5,133},{6,134},{7,135},{8... | collective-permute-start | bytes 393224 | tf_op jit(solution)/shard_map/ppermute | solution.py:31
  29.9 18.5 %collective-permute-start.1 = (bf16[128,1024]{1,0:T(8,128)(2,1)S(1)}, bf16[128,1024]{1,0:T(8,128)(2,1)S(1)}, u32[]{:S(2)}, u32[]{:S(2)}) collective-permute-start(bf16[128,1024]{1,0:T(8,128)(2,1)S(1)} %collective-permute-done.e0), channel_id=1, source_target_pairs={{0,6},{1,7},{2,0},{3,1},{4,2},{5,3},{6,4},{7,5},{8,14},{9,15},{10,... | collective-permute-start | bytes 786440 | tf_op jit(solution)/shard_map/ppermute | solution.py:31
  32.7 15.8 %collective-permute-start.2 = (bf16[128,1024]{1,0:T(8,128)(2,1)S(1)}, bf16[128,1024]{1,0:T(8,128)(2,1)S(1)}, u32[]{:S(2)}, u32[]{:S(2)}) collective-permute-start(bf16[128,1024]{1,0:T(8,128)(2,1)S(1)} %collective-permute-done.e0), channel_id=1, source_target_pairs={{0,4},{1,5},{2,6},{3,7},{4,0},{5,1},{6,2},{7,3},{8,12},{9,13},{10,... | collective-permute-start | bytes 786440 | tf_op jit(solution)/shard_map/ppermute | solution.py:31
  33.5 15.0 %collective-permute-start.3 = (bf16[128,1024]{1,0:T(8,128)(2,1)S(1)}, bf16[128,1024]{1,0:T(8,128)(2,1)S(1)}, u32[]{:S(2)}, u32[]{:S(2)}) collective-permute-start(bf16[128,1024]{1,0:T(8,128)(2,1)S(1)} %collective-permute-done.e0), channel_id=1, source_target_pairs={{0,2},{1,3},{2,4},{3,5},{4,6},{5,7},{6,0},{7,1},{8,10},{9,11},{10,... | collective-permute-start | bytes 786440 | tf_op jit(solution)/shard_map/ppermute | solution.py:31
  34.5 1.0 copy-start
  35.5 0.9 copy-start.3
  36.4 0.7 copy-start.4
  38.1 11.9 %collective-permute-start.13 = (bf16[528,256]{1,0:T(8,128)(2,1)S(1)}, bf16[528,256]{1,0:T(8,128)(2,1)S(1)}, u32[]{:S(2)}, u32[]{:S(2)}) collective-permute-start(bf16[528,256]{1,0:T(8,128)(2,1)S(1)} %project.3.refs_4_), channel_id=1, source_target_pairs={{0,16},{1,17},{2,18},{3,19},{4,20},{5,21},{6,22},{7,23},{8,24},{9,... | collective-permute-start | bytes 811016 | tf_op jit(solution)/shard_map/ppermute | solution.py:31
  41.5 7.0 %collective-permute-start.7 = (bf16[64,1024]{1,0:T(8,128)(2,1)S(1)}, bf16[64,1024]{1,0:T(8,128)(2,1)S(1)}, u32[]{:S(2)}, u32[]{:S(2)}) collective-permute-start(bf16[64,1024]{1,0:T(8,128)(2,1)S(1)} %pad_maximum_fusion.refs_0_), channel_id=1, source_target_pairs={{0,64},{1,65},{2,66},{3,67},{4,68},{5,69},{6,70},{7,71},{8,72},{9,... | collective-permute-start | bytes 393224 | tf_op jit(solution)/shard_map/ppermute | solution.py:31
  48.4 2.8 %collective-permute-start.12 = (bf16[528,256]{1,0:T(8,128)(2,1)S(1)}, bf16[528,256]{1,0:T(8,128)(2,1)S(1)}, u32[]{:S(2)}, u32[]{:S(2)}) collective-permute-start(bf16[528,256]{1,0:T(8,128)(2,1)S(1)} %project.3.refs_4_), channel_id=1, source_target_pairs={{0,8},{1,9},{2,10},{3,11},{4,12},{5,13},{6,14},{7,15},{8,0},{9,1},... | collective-permute-start | bytes 811016 | tf_op jit(solution)/shard_map/ppermute | solution.py:31
  49.5 1.8 %collective-permute-start.15 = (bf16[528,256]{1,0:T(8,128)(2,1)S(1)}, bf16[528,256]{1,0:T(8,128)(2,1)S(1)}, u32[]{:S(2)}, u32[]{:S(2)}) collective-permute-start(bf16[528,256]{1,0:T(8,128)(2,1)S(1)} %project.2.refs_8_), channel_id=1, source_target_pairs={{0,8},{1,9},{2,10},{3,11},{4,12},{5,13},{6,14},{7,15},{8,0},{9,1},... | collective-permute-start | bytes 811016 | tf_op jit(solution)/shard_map/ppermute | solution.py:31
  50.1 1.6 %collective-permute-start.14 = (bf16[528,256]{1,0:T(8,128)(2,1)S(1)}, bf16[528,256]{1,0:T(8,128)(2,1)S(1)}, u32[]{:S(2)}, u32[]{:S(2)}) collective-permute-start(bf16[528,256]{1,0:T(8,128)(2,1)S(1)} %collective-permute-done.13.refs_6_), channel_id=1, source_target_pairs={{0,8},{1,9},{2,10},{3,11},{4,12},{5,13},{6,14},{7,15},{8,0},{9,1},... | collective-permute-start | bytes 811016 | tf_op jit(solution)/shard_map/ppermute | solution.py:31
  50.2 9.3 %collective-permute-start.8 = (bf16[528,256]{1,0:T(8,128)(2,1)S(1)}, bf16[528,256]{1,0:T(8,128)(2,1)S(1)}, u32[]{:S(2)}, u32[]{:S(2)}) collective-permute-start(bf16[528,256]{1,0:T(8,128)(2,1)S(1)} %project.2.refs_8_), channel_id=1, source_target_pairs={{0,16},{1,17},{2,18},{3,19},{4,20},{5,21},{6,22},{7,23},{8,24},{9,... | collective-permute-start | bytes 811016 | tf_op jit(solution)/shard_map/ppermute | solution.py:31
  59.5 1.6 %collective-permute-start.16 = (bf16[528,256]{1,0:T(8,128)(2,1)S(1)}, bf16[528,256]{1,0:T(8,128)(2,1)S(1)}, u32[]{:S(2)}, u32[]{:S(2)}) collective-permute-start(bf16[528,256]{1,0:T(8,128)(2,1)S(1)} %collective-permute-done.8.rest_0_), channel_id=1, source_target_pairs={{0,8},{1,9},{2,10},{3,11},{4,12},{5,13},{6,14},{7,15},{8,0},{9,1},... | collective-permute-start | bytes 811016 | tf_op jit(solution)/shard_map/ppermute | solution.py:31
  62.9 10.6 %collective-permute-start.19 = (bf16[64,1152]{1,0:T(8,128)(2,1)S(1)}, bf16[64,1152]{1,0:T(8,128)(2,1)S(1)}, u32[]{:S(2)}, u32[]{:S(2)}) collective-permute-start(bf16[64,1152]{1,0:T(8,128)(2,1)S(1)} %attend_far.7), channel_id=1, source_target_pairs={{0,192},{1,193},{2,194},{3,195},{4,196},{5,197},{6,198},{7,199},{8... | collective-permute-start | bytes 442376 | tf_op jit(solution)/shard_map/ppermute | solution.py:31
  67.6 7.6 %collective-permute-start.18 = (bf16[64,1152]{1,0:T(8,128)(2,1)S(1)}, bf16[64,1152]{1,0:T(8,128)(2,1)S(1)}, u32[]{:S(2)}, u32[]{:S(2)}) collective-permute-start(bf16[64,1152]{1,0:T(8,128)(2,1)S(1)} %attend_far.6), channel_id=1, source_target_pairs={{0,128},{1,129},{2,130},{3,131},{4,132},{5,133},{6,134},{7,135},{8... | collective-permute-start | bytes 442376 | tf_op jit(solution)/shard_map/ppermute | solution.py:31
  69.7 23.5 %copy-start.2 = (bf16[4,1024,256]{2,1,0:T(8,128)(2,1)S(1)}, bf16[4,1024,256]{2,1,0:T(8,128)(2,1)}, u32[]{:S(2)}) copy-start(bf16[4,1024,256]{2,1,0:T(8,128)(2,1)} %all-gather.2.cloned.1.call-done.weights) | copy-start | bytes 6291460
  69.8 6.4 %collective-permute-start.17 = (bf16[64,1152]{1,0:T(8,128)(2,1)S(1)}, bf16[64,1152]{1,0:T(8,128)(2,1)S(1)}, u32[]{:S(2)}, u32[]{:S(2)}) collective-permute-start(bf16[64,1152]{1,0:T(8,128)(2,1)S(1)} %attend_far.5), channel_id=1, source_target_pairs={{0,64},{1,65},{2,66},{3,67},{4,68},{5,69},{6,70},{7,71},{8,72},{9,... | collective-permute-start | bytes 442376 | tf_op jit(solution)/shard_map/ppermute | solution.py:31
  73.5 48.0 %copy-start.5 = (bf16[128,256]{1,0:T(8,128)(2,1)S(1)}, bf16[128,256]{1,0:T(8,128)(2,1)}, u32[]{:S(2)}) copy-start(bf16[128,256]{1,0:T(8,128)(2,1)} %param.11) | copy-start | bytes 196612
  76.7 9.6 %collective-permute-start.20 = (bf16[64,1152]{1,0:T(8,128)(2,1)S(1)}, bf16[64,1152]{1,0:T(8,128)(2,1)S(1)}, u32[]{:S(2)}, u32[]{:S(2)}) collective-permute-start(bf16[64,1152]{1,0:T(8,128)(2,1)S(1)} %fold.2.refs_0_), channel_id=1, source_target_pairs={{0,32},{1,33},{2,34},{3,35},{4,36},{5,37},{6,38},{7,39},{8,40},{9,... | collective-permute-start | bytes 442376 | tf_op jit(solution)/shard_map/ppermute | solution.py:31
  86.6 5.2 %collective-permute-start.21 = (bf16[64,1024]{1,0:T(8,128)(2,1)S(1)}, bf16[64,1024]{1,0:T(8,128)(2,1)S(1)}, u32[]{:S(2)}, u32[]{:S(2)}) collective-permute-start(bf16[64,1024]{1,0:T(8,128)(2,1)S(1)} %fold.3.r0), channel_id=1, source_target_pairs={{0,16},{1,17},{2,18},{3,19},{4,20},{5,21},{6,22},{7,23},{8,24},{9,... | collective-permute-start | bytes 393224 | tf_op jit(solution)/shard_map/ppermute | solution.py:31
  86.7 5.1 %collective-permute-start.22 = (bf16[64,1024]{1,0:T(8,128)(2,1)S(1)}, bf16[64,1024]{1,0:T(8,128)(2,1)S(1)}, u32[]{:S(2)}, u32[]{:S(2)}) collective-permute-start(bf16[64,1024]{1,0:T(8,128)(2,1)S(1)} %fold.3.r0), channel_id=1, source_target_pairs={{0,8},{1,9},{2,10},{3,11},{4,12},{5,13},{6,14},{7,15},{8,0},{9,1},... | collective-permute-start | bytes 393224 | tf_op jit(solution)/shard_map/ppermute | solution.py:31
  91.9 1.3 %collective-permute-start.23 = (bf16[64,1024]{1,0:T(8,128)(2,1)S(1)}, bf16[64,1024]{1,0:T(8,128)(2,1)S(1)}, u32[]{:S(2)}, u32[]{:S(2)}) collective-permute-start(bf16[64,1024]{1,0:T(8,128)(2,1)S(1)} %collective-permute-done.21.r1), channel_id=1, source_target_pairs={{0,8},{1,9},{2,10},{3,11},{4,12},{5,13},{6,14},{7,15},{8,0},{9,1},... | collective-permute-start | bytes 393224 | tf_op jit(solution)/shard_map/ppermute | solution.py:31
  94.5 9.1 %collective-permute-start.24 = (bf16[256,256]{1,0:T(8,128)(2,1)S(1)}, bf16[256,256]{1,0:T(8,128)(2,1)S(1)}, u32[]{:S(2)}, u32[]{:S(2)}) collective-permute-start(bf16[256,256]{1,0:T(8,128)(2,1)S(1)} %get-tuple-element.35), channel_id=1, source_target_pairs={{0,0},{1,1},{2,2},{3,3},{4,4},{5,5},{6,6},{7,7},{8,8},{9,9},{10,10... | collective-permute-start | bytes 393224 | tf_op jit(solution)/shard_map/ppermute | solution.py:31
  97.7 7.2 %collective-permute-start.25 = (bf16[256,256]{1,0:T(8,128)(2,1)S(1)}, bf16[256,256]{1,0:T(8,128)(2,1)S(1)}, u32[]{:S(2)}, u32[]{:S(2)}) collective-permute-start(bf16[256,256]{1,0:T(8,128)(2,1)S(1)} %get-tuple-element.36), channel_id=1, source_target_pairs={{0,64},{1,65},{2,66},{3,67},{4,68},{5,69},{6,70},{7,71},{8,72},{9,... | collective-permute-start | bytes 393224 | tf_op jit(solution)/shard_map/ppermute | solution.py:31
  101.0 8.8 %collective-permute-start.26 = (bf16[256,256]{1,0:T(8,128)(2,1)S(1)}, bf16[256,256]{1,0:T(8,128)(2,1)S(1)}, u32[]{:S(2)}, u32[]{:S(2)}) collective-permute-start(bf16[256,256]{1,0:T(8,128)(2,1)S(1)} %get-tuple-element.37), channel_id=1, source_target_pairs={{0,128},{1,129},{2,130},{3,131},{4,132},{5,133},{6,134},{7,135},{8... | collective-permute-start | bytes 393224 | tf_op jit(solution)/shard_map/ppermute | solution.py:31
  101.2 11.4 %collective-permute-start.27 = (bf16[256,256]{1,0:T(8,128)(2,1)S(1)}, bf16[256,256]{1,0:T(8,128)(2,1)S(1)}, u32[]{:S(2)}, u32[]{:S(2)}) collective-permute-start(bf16[256,256]{1,0:T(8,128)(2,1)S(1)} %get-tuple-element.38), channel_id=1, source_target_pairs={{0,192},{1,193},{2,194},{3,195},{4,196},{5,197},{6,198},{7,199},{8... | collective-permute-start | bytes 393224 | tf_op jit(solution)/shard_map/ppermute | solution.py:31
  113.2 8.3 %collective-permute-start.28 = (bf16[128,256]{1,0:T(8,128)(2,1)S(1)}, bf16[128,256]{1,0:T(8,128)(2,1)S(1)}, u32[]{:S(2)}, u32[]{:S(2)}) collective-permute-start(bf16[128,256]{1,0:T(8,128)(2,1)S(1)} %get-tuple-element.40), channel_id=1, source_target_pairs={{0,1},{1,0},{2,3},{3,2},{4,5},{5,4},{6,7},{7,6},{8,9},{9,8},{10,11... | collective-permute-start | bytes 196616 | tf_op jit(solution)/shard_map/ppermute | solution.py:31
Sparse Core Ops, SparseCore 0:
  9.2 39.4 all-gather.1

commit v3 on v2

--- a/solution.py
+++ b/solution.py
@@ -57,6 +57,7 @@
 
 ANY = pl.BlockSpec(memory_space=pl.ANY)
 SMEM = pl.BlockSpec(memory_space=pltpu.SMEM)
+OWN_COPIES = pltpu.CompilerParams(vmem_limit_bytes=60 * 1024 * 1024)
 PARAMS = pltpu.CompilerParams(vmem_limit_bytes=40 * 1024 * 1024)
 
 
@@ -98,7 +99,7 @@
         out_shape=jax.ShapeDtypeStruct((528, 2 * HD), bf16),
         in_specs=[SMEM, SMEM] + vmem(5) + [ANY] * len(after),
         out_specs=vmem(1)[0],
-        compiler_params=PARAMS,
+        compiler_params=PARAMS if flip else OWN_COPIES,
         cost_estimate=cost(2 * 512 * 1024 * 256, 2 << 20) if flip else cost(1024, 1024),
         name="project",
     )(place, lens, *blocks, weight, *after)

time: 130 us -> 131 us (level)
  waiting for transfers between devices: 42.4 us -> 44.8 us
  starting transfers between devices: 49 us -> 47.3 us
  Pallas kernels: 19.8 us -> 21.3 us
    ppermute x29, waiting for transfers between devices: 41.6 us -> 44.1 us  [move(): return lax.ppermute(value, AXES, pairs)]
    ppermute x29, starting transfers between devices: 49 us -> 47.3 us  [move(): return lax.ppermute(value, AXES, pairs)]
    pallas_call x2, Pallas kernels: 2 us -> 3.57 us  [project(): pl.pallas_call(functools.partial(project_kernel, flip), out_shape=jax.Sha...]
    unnamed x12 -> x20, local copies, waits for them, and re-layouts: 2.66 us -> 1.64 us
  transfers between devices with their start and end apart: 30 -> 30, of which waited for: 13 -> 15; matrix products, arithmetic and copies ran while one was open for 1% -> 1% of each run, Pallas kernels for 12% -> 13%
where the time goes in v3:
time: 131 us
  starting transfers between devices  47.3 us (36%)
  waiting for transfers between devices  44.8 us (34%)
  Pallas kernels  21.3 us (16%)
  between operations  13.6 us (10%)
  local copies, waits for them, and re-layouts  2.3 us (2%)
  other arithmetic  1.51 us (1%)
    ppermute x29, starting transfers between devices, move(): return lax.ppermute(value, AXES, pairs)  47.3 us
    ppermute x29, waiting for transfers between devices, move(): return lax.ppermute(value, AXES, pairs)  44.1 us
    pallas_call x1, Pallas kernels, attend_near(): pl.pallas_call(near_kernel, out_shape=(jax.ShapeDtypeStruct((4, count, GR...  7.79 us
    pallas_call x4, Pallas kernels, attend_far(): pl.pallas_call(functools.partial(far_kernel, k), out_shape=jax.ShapeDtype...  7.13 us
    pallas_call x2, Pallas kernels, project(): pl.pallas_call(functools.partial(project_kernel, flip), out_shape=jax.Sha...  3.57 us
  transfers between devices with their start and end apart: 30, of which 15 were waited for; matrix products, arithmetic and copies ran while one was open for 1% of the time, Pallas kernels for 13%

profile of v3, /device:TPU:8, one launch (start us, length us, event | category | flops | bytes accessed | tf_op | source)
XLA Modules:
  0.0 130.8 jit_solution(15675389393610280479)
XLA Ops:
  6.5 0.7 all-gather.2.cloned.1.call-update
  7.3 3.4 %collective-permute-start.4 = (bf16[32,1024]{1,0:T(8,128)(2,1)}, bf16[32,1024]{1,0:T(8,128)(2,1)S(1)}, u32[]{:S(2)}, u32[]{:S(2)}) collective-permute-start(bf16[32,1024]{1,0:T(8,128)(2,1)} %bitcast.9), channel_id=1, source_target_pairs={{0,32},{1,33},{2,34},{3,35},{4,36},{5,37},{6,38},{7,39},{8,40},{9,... | collective-permute-start | bytes 196616 | tf_op jit(solution)/shard_map/ppermute | solution.py:31
  10.6 5.4 %collective-permute-start = (bf16[128,1024]{1,0:T(8,128)(2,1)}, bf16[128,1024]{1,0:T(8,128)(2,1)S(1)}, u32[]{:S(2)}, u32[]{:S(2)}) collective-permute-start(bf16[128,1024]{1,0:T(8,128)(2,1)} %e0.1), channel_id=1, source_target_pairs={{0,1},{1,0},{2,3},{3,2},{4,5},{5,4},{6,7},{7,6},{8,9},{9,8},{10,11... | collective-permute-start | bytes 786440 | tf_op jit(solution)/shard_map/ppermute | solution.py:31
  16.0 3.0 %collective-permute-start.10 = (bf16[128,1024]{1,0:T(8,128)(2,1)}, bf16[128,1024]{1,0:T(8,128)(2,1)S(1)}, u32[]{:S(2)}, u32[]{:S(2)}) collective-permute-start(bf16[128,1024]{1,0:T(8,128)(2,1)} %e0.1), channel_id=1, source_target_pairs={{0,4},{1,5},{2,6},{3,7},{4,0},{5,1},{6,2},{7,3},{8,12},{9,13},{10,... | collective-permute-start | bytes 786440 | tf_op jit(solution)/shard_map/ppermute | solution.py:31
  19.0 0.6 collective-permute-start.11
  19.6 2.6 %collective-permute-start.9 = (bf16[128,1024]{1,0:T(8,128)(2,1)}, bf16[128,1024]{1,0:T(8,128)(2,1)S(1)}, u32[]{:S(2)}, u32[]{:S(2)}) collective-permute-start(bf16[128,1024]{1,0:T(8,128)(2,1)} %e0.1), channel_id=1, source_target_pairs={{0,6},{1,7},{2,0},{3,1},{4,2},{5,3},{6,4},{7,5},{8,14},{9,15},{10,... | collective-permute-start | bytes 786440 | tf_op jit(solution)/shard_map/ppermute | solution.py:31
  22.3 0.8 pad_maximum_fusion.refs_0_
  23.1 0.5 collective-permute-start.5
  23.7 4.0 %collective-permute-done.e0 = bf16[128,1024]{1,0:T(8,128)(2,1)S(1)} collective-permute-done((bf16[128,1024]{1,0:T(8,128)(2,1)}, bf16[128,1024]{1,0:T(8,128)(2,1)S(1)}, u32[]{:S(2)}, u32[]{:S(2)}) %collective-permute-start) | collective-permute-done | bytes 262176 | tf_op jit(solution)/shard_map/ppermute | solution.py:31
  27.6 2.3 %collective-permute-start.6 = (bf16[64,1024]{1,0:T(8,128)(2,1)S(1)}, bf16[64,1024]{1,0:T(8,128)(2,1)S(1)}, u32[]{:S(2)}, u32[]{:S(2)}) collective-permute-start(bf16[64,1024]{1,0:T(8,128)(2,1)S(1)} %pad_maximum_fusion.refs_0_), channel_id=1, source_target_pairs={{0,128},{1,129},{2,130},{3,131},{4,132},{5,133},{6,134},{7,135},{8... | collective-permute-start | bytes 393224 | tf_op jit(solution)/shard_map/ppermute | solution.py:31
  29.9 2.8 %collective-permute-start.1 = (bf16[128,1024]{1,0:T(8,128)(2,1)S(1)}, bf16[128,1024]{1,0:T(8,128)(2,1)S(1)}, u32[]{:S(2)}, u32[]{:S(2)}) collective-permute-start(bf16[128,1024]{1,0:T(8,128)(2,1)S(1)} %collective-permute-done.e0), channel_id=1, source_target_pairs={{0,6},{1,7},{2,0},{3,1},{4,2},{5,3},{6,4},{7,5},{8,14},{9,15},{10,... | collective-permute-start | bytes 786440 | tf_op jit(solution)/shard_map/ppermute | solution.py:31
  32.7 0.8 collective-permute-start.2
  33.5 0.9 collective-permute-start.3
  34.4 0.7 stack.23.place_ref
  35.1 2.6 %project.3.refs_4_ = bf16[528,256]{1,0:T(8,128)(2,1)} custom-call(s32[5]{0:T(128)} %stack.23.place_ref, s32[16]{0:T(128)} %lens_ref.3, bf16[128,1024]{1,0:T(8,128)(2,1)} %e0.1, bf16[128,1024]{1,0:T(8,128)(2,1)} %copy-done.8, bf16[128,1024]{1,0:T(8,128)(2,1)} %copy-done.6, bf16[128,1024]{1,0:T(8,128)(2,1)} %copy-done.7, bf16[1024,256]{1,0:T(8,128)(2,1)} %bitcast.7), custom_call_target="tpu_custom_call" | custom-call | flops 1024 | bytes 1024 | tf_op jit(solution)/shard_map/project/pallas_call | solution.py:97
  37.6 3.3 %collective-permute-start.13 = (bf16[528,256]{1,0:T(8,128)(2,1)}, bf16[528,256]{1,0:T(8,128)(2,1)S(1)}, u32[]{:S(2)}, u32[]{:S(2)}) collective-permute-start(bf16[528,256]{1,0:T(8,128)(2,1)} %project.3.refs_4_), channel_id=1, source_target_pairs={{0,16},{1,17},{2,18},{3,19},{4,20},{5,21},{6,22},{7,23},{8,24},{9,... | collective-permute-start | bytes 811016 | tf_op jit(solution)/shard_map/ppermute | solution.py:31
  40.9 7.4 %collective-permute-done.7.refs_3_ = bf16[64,1024]{1,0:T(8,128)(2,1)S(1)} collective-permute-done((bf16[64,1024]{1,0:T(8,128)(2,1)S(1)}, bf16[64,1024]{1,0:T(8,128)(2,1)S(1)}, u32[]{:S(2)}, u32[]{:S(2)}) %collective-permute-start.7) | collective-permute-done | bytes 131104 | tf_op jit(solution)/shard_map/ppermute | solution.py:31
  48.4 0.7 copy-done.3
  49.0 1.0 project.2.refs_8_
  50.1 0.6 collective-permute-start.15
  50.7 0.7 collective-permute-start.8
  52.2 1.0 copy-done.2
  53.2 7.8 %attend_near.1 = (bf16[4,64,1024]{2,1,0:T(8,128)(2,1)S(1)}, f32[4,64,1024]{2,1,0:T(8,128)S(1)}, f32[4,64,128]{2,1,0:T(8,128)S(1)}) custom-call(bf16[64,1024]{1,0:T(8,128)(2,1)S(1)} %pad_maximum_fusion.refs_0_, bf16[64,1024]{1,0:T(8,128)(2,1)S(1)} %collective-permute-done.5.refs_1_, bf16[64,1024]{1,0:T(8,128)(2,1)S(1)} %collective-permute-done.6.refs_2_, ...), custom_call_target="tpu_custom_call" | custom-call | flops 1024 | bytes 1024 | tf_op jit(solution)/shard_map/attend_near/pallas_call | solution.py:210
  61.4 1.2 collective-permute-done.16.rest_1_
  62.6 1.8 %attend_far.7 = bf16[64,1152]{1,0:T(8,128)(2,1)S(1)} custom-call(s32[5]{0:T(128)S(1)} %copy-done.4, bf16[4,64,1024]{2,1,0:T(8,128)(2,1)S(1)} %get-tuple-element.30.q_all, f32[4,64,1024]{2,1,0:T(8,128)S(1)} %get-tuple-element.31.sums_all, f32[4,64,128]{2,1,0:T(8,128)S(1)} %get-tuple-element.32.stats_all, bf16[528,256]{1,0:T(8,128)(2,1)S(1)} %collective-permute-done.8.rest_0_, ...), custom_call_target="tpu_custom_call" | custom-call | flops 536870912 | bytes 2097152 | tf_op jit(solution)/shard_map/attend_far/pallas_call | solution.py:243
  64.4 2.9 %collective-permute-start.19 = (bf16[64,1152]{1,0:T(8,128)(2,1)S(1)}, bf16[64,1152]{1,0:T(8,128)(2,1)S(1)}, u32[]{:S(2)}, u32[]{:S(2)}) collective-permute-start(bf16[64,1152]{1,0:T(8,128)(2,1)S(1)} %attend_far.7), channel_id=1, source_target_pairs={{0,192},{1,193},{2,194},{3,195},{4,196},{5,197},{6,198},{7,199},{8... | collective-permute-start | bytes 442376 | tf_op jit(solution)/shard_map/ppermute | solution.py:31
  67.3 1.8 %attend_far.6 = bf16[64,1152]{1,0:T(8,128)(2,1)S(1)} custom-call(s32[5]{0:T(128)S(1)} %copy-done.4, bf16[4,64,1024]{2,1,0:T(8,128)(2,1)S(1)} %get-tuple-element.30.q_all, f32[4,64,1024]{2,1,0:T(8,128)S(1)} %get-tuple-element.31.sums_all, f32[4,64,128]{2,1,0:T(8,128)S(1)} %get-tuple-element.32.stats_all, bf16[528,256]{1,0:T(8,128)(2,1)S(1)} %collective-permute-done.8.rest_0_, ...), custom_call_target="tpu_custom_call" | custom-call | flops 536870912 | bytes 2097152 | tf_op jit(solution)/shard_map/attend_far/pallas_call | solution.py:243
  69.4 1.8 %attend_far.5 = bf16[64,1152]{1,0:T(8,128)(2,1)S(1)} custom-call(s32[5]{0:T(128)S(1)} %copy-done.4, bf16[4,64,1024]{2,1,0:T(8,128)(2,1)S(1)} %get-tuple-element.30.q_all, f32[4,64,1024]{2,1,0:T(8,128)S(1)} %get-tuple-element.31.sums_all, f32[4,64,128]{2,1,0:T(8,128)S(1)} %get-tuple-element.32.stats_all, bf16[528,256]{1,0:T(8,128)(2,1)S(1)} %collective-permute-done.8.rest_0_, ...), custom_call_target="tpu_custom_call" | custom-call | flops 536870912 | bytes 2097152 | tf_op jit(solution)/shard_map/attend_far/pallas_call | solution.py:243
  71.2 1.5 %collective-permute-start.17 = (bf16[64,1152]{1,0:T(8,128)(2,1)S(1)}, bf16[64,1152]{1,0:T(8,128)(2,1)S(1)}, u32[]{:S(2)}, u32[]{:S(2)}) collective-permute-start(bf16[64,1152]{1,0:T(8,128)(2,1)S(1)} %attend_far.5), channel_id=1, source_target_pairs={{0,64},{1,65},{2,66},{3,67},{4,68},{5,69},{6,70},{7,71},{8,72},{9,... | collective-permute-start | bytes 442376 | tf_op jit(solution)/shard_map/ppermute | solution.py:31
  72.8 1.8 %attend_far.4.refs_0_ = bf16[64,1152]{1,0:T(8,128)(2,1)S(1)} custom-call(s32[5]{0:T(128)S(1)} %copy-done.4, bf16[4,64,1024]{2,1,0:T(8,128)(2,1)S(1)} %get-tuple-element.30.q_all, f32[4,64,1024]{2,1,0:T(8,128)S(1)} %get-tuple-element.31.sums_all, f32[4,64,128]{2,1,0:T(8,128)S(1)} %get-tuple-element.32.stats_all, ...), custom_call_target="tpu_custom_call" | custom-call | flops 536870912 | bytes 2097152 | tf_op jit(solution)/shard_map/attend_far/pallas_call | solution.py:243
  74.6 2.2 %collective-permute-done.18.refs_2_ = bf16[64,1152]{1,0:T(8,128)(2,1)S(1)} collective-permute-done((bf16[64,1152]{1,0:T(8,128)(2,1)S(1)}, bf16[64,1152]{1,0:T(8,128)(2,1)S(1)}, u32[]{:S(2)}, u32[]{:S(2)}) %collective-permute-start.18) | collective-permute-done | bytes 147488 | tf_op jit(solution)/shard_map/ppermute | solution.py:31
  76.8 0.9 collective-permute-done.17.refs_1_
  77.7 0.5 fold.2.refs_0_
  78.2 0.5 collective-permute-start.20
  78.7 8.9 %collective-permute-done.20.refs_1_ = bf16[64,1152]{1,0:T(8,128)(2,1)S(1)} collective-permute-done((bf16[64,1152]{1,0:T(8,128)(2,1)S(1)}, bf16[64,1152]{1,0:T(8,128)(2,1)S(1)}, u32[]{:S(2)}, u32[]{:S(2)}) %collective-permute-start.20) | collective-permute-done | bytes 147488 | tf_op jit(solution)/shard_map/ppermute | solution.py:31
  88.2 5.3 %collective-permute-done.21.r1 = bf16[64,1024]{1,0:T(8,128)(2,1)S(1)} collective-permute-done((bf16[64,1024]{1,0:T(8,128)(2,1)S(1)}, bf16[64,1024]{1,0:T(8,128)(2,1)S(1)}, u32[]{:S(2)}, u32[]{:S(2)}) %collective-permute-start.21) | collective-permute-done | bytes 131104 | tf_op jit(solution)/shard_map/ppermute | solution.py:31
  93.5 1.3 %collective-permute-done.23.r3 = bf16[64,1024]{1,0:T(8,128)(2,1)S(1)} collective-permute-done((bf16[64,1024]{1,0:T(8,128)(2,1)S(1)}, bf16[64,1024]{1,0:T(8,128)(2,1)S(1)}, u32[]{:S(2)}, u32[]{:S(2)}) %collective-permute-start.23) | collective-permute-done | bytes 131104 | tf_op jit(solution)/shard_map/ppermute | solution.py:31
  94.8 1.3 output.1
  96.1 3.6 %collective-permute-start.24 = (bf16[256,256]{1,0:T(8,128)(2,1)S(1)}, bf16[256,256]{1,0:T(8,128)(2,1)S(1)}, u32[]{:S(2)}, u32[]{:S(2)}) collective-permute-start(bf16[256,256]{1,0:T(8,128)(2,1)S(1)} %get-tuple-element.35), channel_id=1, source_target_pairs={{0,0},{1,1},{2,2},{3,3},{4,4},{5,5},{6,6},{7,7},{8,8},{9,9},{10,10... | collective-permute-start | bytes 393224 | tf_op jit(solution)/shard_map/ppermute | solution.py:31
  99.7 2.7 %collective-permute-start.25 = (bf16[256,256]{1,0:T(8,128)(2,1)S(1)}, bf16[256,256]{1,0:T(8,128)(2,1)S(1)}, u32[]{:S(2)}, u32[]{:S(2)}) collective-permute-start(bf16[256,256]{1,0:T(8,128)(2,1)S(1)} %get-tuple-element.36), channel_id=1, source_target_pairs={{0,64},{1,65},{2,66},{3,67},{4,68},{5,69},{6,70},{7,71},{8,72},{9,... | collective-permute-start | bytes 393224 | tf_op jit(solution)/shard_map/ppermute | solution.py:31
  102.5 2.4 %collective-permute-start.27 = (bf16[256,256]{1,0:T(8,128)(2,1)S(1)}, bf16[256,256]{1,0:T(8,128)(2,1)S(1)}, u32[]{:S(2)}, u32[]{:S(2)}) collective-permute-start(bf16[256,256]{1,0:T(8,128)(2,1)S(1)} %get-tuple-element.38), channel_id=1, source_target_pairs={{0,192},{1,193},{2,194},{3,195},{4,196},{5,197},{6,198},{7,199},{8... | collective-permute-start | bytes 393224 | tf_op jit(solution)/shard_map/ppermute | solution.py:31
  105.0 2.1 %collective-permute-done.25.t1 = bf16[256,256]{1,0:T(8,128)(2,1)S(1)} collective-permute-done((bf16[256,256]{1,0:T(8,128)(2,1)S(1)}, bf16[256,256]{1,0:T(8,128)(2,1)S(1)}, u32[]{:S(2)}, u32[]{:S(2)}) %collective-permute-start.25) | collective-permute-done | bytes 131104 | tf_op jit(solution)/shard_map/ppermute | solution.py:31
  107.1 4.2 %collective-permute-done.26.t2 = bf16[256,256]{1,0:T(8,128)(2,1)S(1)} collective-permute-done((bf16[256,256]{1,0:T(8,128)(2,1)S(1)}, bf16[256,256]{1,0:T(8,128)(2,1)S(1)}, u32[]{:S(2)}, u32[]{:S(2)}) %collective-permute-start.26) | collective-permute-done | bytes 131104 | tf_op jit(solution)/shard_map/ppermute | solution.py:31
  111.3 3.2 %collective-permute-done.27.t3 = bf16[256,256]{1,0:T(8,128)(2,1)S(1)} collective-permute-done((bf16[256,256]{1,0:T(8,128)(2,1)S(1)}, bf16[256,256]{1,0:T(8,128)(2,1)S(1)}, u32[]{:S(2)}, u32[]{:S(2)}) %collective-permute-start.27) | collective-permute-done | bytes 131104 | tf_op jit(solution)/shard_map/ppermute | solution.py:31
  114.5 0.6 sum_terms.1
  115.1 5.8 %collective-permute-start.28 = (bf16[128,256]{1,0:T(8,128)(2,1)S(1)}, bf16[128,256]{1,0:T(8,128)(2,1)S(1)}, u32[]{:S(2)}, u32[]{:S(2)}) collective-permute-start(bf16[128,256]{1,0:T(8,128)(2,1)S(1)} %get-tuple-element.40), channel_id=1, source_target_pairs={{0,1},{1,0},{2,3},{3,2},{4,5},{5,4},{6,7},{7,6},{8,9},{9,8},{10,11... | collective-permute-start | bytes 196616 | tf_op jit(solution)/shard_map/ppermute | solution.py:31
  120.8 2.5 %collective-permute-done.28 = bf16[128,256]{1,0:T(8,128)(2,1)S(1)} collective-permute-done((bf16[128,256]{1,0:T(8,128)(2,1)S(1)}, bf16[128,256]{1,0:T(8,128)(2,1)S(1)}, u32[]{:S(2)}, u32[]{:S(2)}) %collective-permute-start.28) | collective-permute-done | bytes 65568 | tf_op jit(solution)/shard_map/ppermute | solution.py:31
  123.3 0.7 add_convert_fusion
  (47 shorter events, 2.5 us)
Async XLA Ops:
  6.5 41.8 %copy-start = (bf16[1024,1,256]{2,0,1:T(8,128)(2,1)S(1)}, bf16[1024,1,256]{2,0,1:T(8,128)(2,1)}, u32[]{:S(2)}) copy-start(bf16[1024,1,256]{2,0,1:T(8,128)(2,1)} %param.8) | copy-start | bytes 1572868
  6.5 41.8 %copy-start.5 = (s32[16]{0:T(128)S(1)}, s32[16]{0:T(128)}, u32[]{:S(2)}) copy-start(s32[16]{0:T(128)} %lens_ref.3) | copy-start | bytes 196
  6.5 54.4 %all-gather.2.cloned.1.call-start = ((), (), s32[]{:S(2)}) async-start(), calls=%async_computation | async-start | bytes 2621440 | tf_op jit(solution)/shard_map/all_gather | solution.py:344
  7.3 15.0 %collective-permute-start.4 = (bf16[32,1024]{1,0:T(8,128)(2,1)}, bf16[32,1024]{1,0:T(8,128)(2,1)S(1)}, u32[]{:S(2)}, u32[]{:S(2)}) collective-permute-start(bf16[32,1024]{1,0:T(8,128)(2,1)} %bitcast.9), channel_id=1, source_target_pairs={{0,32},{1,33},{2,34},{3,35},{4,36},{5,37},{6,38},{7,39},{8,40},{9,... | collective-permute-start | bytes 196616 | tf_op jit(solution)/shard_map/ppermute | solution.py:31
  10.6 17.0 %collective-permute-start = (bf16[128,1024]{1,0:T(8,128)(2,1)}, bf16[128,1024]{1,0:T(8,128)(2,1)S(1)}, u32[]{:S(2)}, u32[]{:S(2)}) collective-permute-start(bf16[128,1024]{1,0:T(8,128)(2,1)} %e0.1), channel_id=1, source_target_pairs={{0,1},{1,0},{2,3},{3,2},{4,5},{5,4},{6,7},{7,6},{8,9},{9,8},{10,11... | collective-permute-start | bytes 786440 | tf_op jit(solution)/shard_map/ppermute | solution.py:31
  16.0 13.9 %collective-permute-start.10 = (bf16[128,1024]{1,0:T(8,128)(2,1)}, bf16[128,1024]{1,0:T(8,128)(2,1)S(1)}, u32[]{:S(2)}, u32[]{:S(2)}) collective-permute-start(bf16[128,1024]{1,0:T(8,128)(2,1)} %e0.1), channel_id=1, source_target_pairs={{0,4},{1,5},{2,6},{3,7},{4,0},{5,1},{6,2},{7,3},{8,12},{9,13},{10,... | collective-permute-start | bytes 786440 | tf_op jit(solution)/shard_map/ppermute | solution.py:31
  19.0 13.7 %collective-permute-start.11 = (bf16[128,1024]{1,0:T(8,128)(2,1)}, bf16[128,1024]{1,0:T(8,128)(2,1)S(1)}, u32[]{:S(2)}, u32[]{:S(2)}) collective-permute-start(bf16[128,1024]{1,0:T(8,128)(2,1)} %e0.1), channel_id=1, source_target_pairs={{0,2},{1,3},{2,4},{3,5},{4,6},{5,7},{6,0},{7,1},{8,10},{9,11},{10,... | collective-permute-start | bytes 786440 | tf_op jit(solution)/shard_map/ppermute | solution.py:31
  19.6 13.9 %collective-permute-start.9 = (bf16[128,1024]{1,0:T(8,128)(2,1)}, bf16[128,1024]{1,0:T(8,128)(2,1)S(1)}, u32[]{:S(2)}, u32[]{:S(2)}) collective-permute-start(bf16[128,1024]{1,0:T(8,128)(2,1)} %e0.1), channel_id=1, source_target_pairs={{0,6},{1,7},{2,0},{3,1},{4,2},{5,3},{6,4},{7,5},{8,14},{9,15},{10,... | collective-permute-start | bytes 786440 | tf_op jit(solution)/shard_map/ppermute | solution.py:31
  23.1 14.5 %collective-permute-start.5 = (bf16[64,1024]{1,0:T(8,128)(2,1)S(1)}, bf16[64,1024]{1,0:T(8,128)(2,1)S(1)}, u32[]{:S(2)}, u32[]{:S(2)}) collective-permute-start(bf16[64,1024]{1,0:T(8,128)(2,1)S(1)} %pad_maximum_fusion.refs_0_), channel_id=1, source_target_pairs={{0,192},{1,193},{2,194},{3,195},{4,196},{5,197},{6,198},{7,199},{8... | collective-permute-start | bytes 393224 | tf_op jit(solution)/shard_map/ppermute | solution.py:31
  27.6 13.3 %collective-permute-start.6 = (bf16[64,1024]{1,0:T(8,128)(2,1)S(1)}, bf16[64,1024]{1,0:T(8,128)(2,1)S(1)}, u32[]{:S(2)}, u32[]{:S(2)}) collective-permute-start(bf16[64,1024]{1,0:T(8,128)(2,1)S(1)} %pad_maximum_fusion.refs_0_), channel_id=1, source_target_pairs={{0,128},{1,129},{2,130},{3,131},{4,132},{5,133},{6,134},{7,135},{8... | collective-permute-start | bytes 393224 | tf_op jit(solution)/shard_map/ppermute | solution.py:31
  29.9 5.1 %copy-start.6 = (bf16[128,1024]{1,0:T(8,128)(2,1)}, bf16[128,1024]{1,0:T(8,128)(2,1)S(1)}, u32[]{:S(2)}) copy-start(bf16[128,1024]{1,0:T(8,128)(2,1)S(1)} %collective-permute-done.10.e2) | copy-start | bytes 786436
  29.9 18.4 %collective-permute-start.1 = (bf16[128,1024]{1,0:T(8,128)(2,1)S(1)}, bf16[128,1024]{1,0:T(8,128)(2,1)S(1)}, u32[]{:S(2)}, u32[]{:S(2)}) collective-permute-start(bf16[128,1024]{1,0:T(8,128)(2,1)S(1)} %collective-permute-done.e0), channel_id=1, source_target_pairs={{0,6},{1,7},{2,0},{3,1},{4,2},{5,3},{6,4},{7,5},{8,14},{9,15},{10,... | collective-permute-start | bytes 786440 | tf_op jit(solution)/shard_map/ppermute | solution.py:31
  32.7 2.4 %copy-start.7 = (bf16[128,1024]{1,0:T(8,128)(2,1)}, bf16[128,1024]{1,0:T(8,128)(2,1)S(1)}, u32[]{:S(2)}) copy-start(bf16[128,1024]{1,0:T(8,128)(2,1)S(1)} %collective-permute-done.11.e3) | copy-start | bytes 786436
  32.7 15.7 %collective-permute-start.2 = (bf16[128,1024]{1,0:T(8,128)(2,1)S(1)}, bf16[128,1024]{1,0:T(8,128)(2,1)S(1)}, u32[]{:S(2)}, u32[]{:S(2)}) collective-permute-start(bf16[128,1024]{1,0:T(8,128)(2,1)S(1)} %collective-permute-done.e0), channel_id=1, source_target_pairs={{0,4},{1,5},{2,6},{3,7},{4,0},{5,1},{6,2},{7,3},{8,12},{9,13},{10,... | collective-permute-start | bytes 786440 | tf_op jit(solution)/shard_map/ppermute | solution.py:31
  33.5 1.6 %copy-start.8 = (bf16[128,1024]{1,0:T(8,128)(2,1)}, bf16[128,1024]{1,0:T(8,128)(2,1)S(1)}, u32[]{:S(2)}) copy-start(bf16[128,1024]{1,0:T(8,128)(2,1)S(1)} %collective-permute-done.9.e1) | copy-start | bytes 786436
  33.5 14.9 %collective-permute-start.3 = (bf16[128,1024]{1,0:T(8,128)(2,1)S(1)}, bf16[128,1024]{1,0:T(8,128)(2,1)S(1)}, u32[]{:S(2)}, u32[]{:S(2)}) collective-permute-start(bf16[128,1024]{1,0:T(8,128)(2,1)S(1)} %collective-permute-done.e0), channel_id=1, source_target_pairs={{0,2},{1,3},{2,4},{3,5},{4,6},{5,7},{6,0},{7,1},{8,10},{9,11},{10,... | collective-permute-start | bytes 786440 | tf_op jit(solution)/shard_map/ppermute | solution.py:31
  35.0 27.6 %copy-start.4 = (s32[5]{0:T(128)S(1)}, s32[5]{0:T(128)}, u32[]{:S(2)}) copy-start(s32[5]{0:T(128)} %stack.23.place_ref) | copy-start | bytes 64
  37.6 13.0 %collective-permute-start.13 = (bf16[528,256]{1,0:T(8,128)(2,1)}, bf16[528,256]{1,0:T(8,128)(2,1)S(1)}, u32[]{:S(2)}, u32[]{:S(2)}) collective-permute-start(bf16[528,256]{1,0:T(8,128)(2,1)} %project.3.refs_4_), channel_id=1, source_target_pairs={{0,16},{1,17},{2,18},{3,19},{4,20},{5,21},{6,22},{7,23},{8,24},{9,... | collective-permute-start | bytes 811016 | tf_op jit(solution)/shard_map/ppermute | solution.py:31
  40.9 7.5 %collective-permute-start.7 = (bf16[64,1024]{1,0:T(8,128)(2,1)S(1)}, bf16[64,1024]{1,0:T(8,128)(2,1)S(1)}, u32[]{:S(2)}, u32[]{:S(2)}) collective-permute-start(bf16[64,1024]{1,0:T(8,128)(2,1)S(1)} %pad_maximum_fusion.refs_0_), channel_id=1, source_target_pairs={{0,64},{1,65},{2,66},{3,67},{4,68},{5,69},{6,70},{7,71},{8,72},{9,... | collective-permute-start | bytes 393224 | tf_op jit(solution)/shard_map/ppermute | solution.py:31
  48.3 3.1 %collective-permute-start.12 = (bf16[528,256]{1,0:T(8,128)(2,1)}, bf16[528,256]{1,0:T(8,128)(2,1)S(1)}, u32[]{:S(2)}, u32[]{:S(2)}) collective-permute-start(bf16[528,256]{1,0:T(8,128)(2,1)} %project.3.refs_4_), channel_id=1, source_target_pairs={{0,8},{1,9},{2,10},{3,11},{4,12},{5,13},{6,14},{7,15},{8,0},{9,1},... | collective-permute-start | bytes 811016 | tf_op jit(solution)/shard_map/ppermute | solution.py:31
  48.4 0.7 copy-start.3
  50.1 1.8 %collective-permute-start.15 = (bf16[528,256]{1,0:T(8,128)(2,1)S(1)}, bf16[528,256]{1,0:T(8,128)(2,1)S(1)}, u32[]{:S(2)}, u32[]{:S(2)}) collective-permute-start(bf16[528,256]{1,0:T(8,128)(2,1)S(1)} %project.2.refs_8_), channel_id=1, source_target_pairs={{0,8},{1,9},{2,10},{3,11},{4,12},{5,13},{6,14},{7,15},{8,0},{9,1},... | collective-permute-start | bytes 811016 | tf_op jit(solution)/shard_map/ppermute | solution.py:31
  50.6 1.6 %collective-permute-start.14 = (bf16[528,256]{1,0:T(8,128)(2,1)S(1)}, bf16[528,256]{1,0:T(8,128)(2,1)S(1)}, u32[]{:S(2)}, u32[]{:S(2)}) collective-permute-start(bf16[528,256]{1,0:T(8,128)(2,1)S(1)} %collective-permute-done.13.refs_6_), channel_id=1, source_target_pairs={{0,8},{1,9},{2,10},{3,11},{4,12},{5,13},{6,14},{7,15},{8,0},{9,1},... | collective-permute-start | bytes 811016 | tf_op jit(solution)/shard_map/ppermute | solution.py:31
  50.7 10.2 %collective-permute-start.8 = (bf16[528,256]{1,0:T(8,128)(2,1)S(1)}, bf16[528,256]{1,0:T(8,128)(2,1)S(1)}, u32[]{:S(2)}, u32[]{:S(2)}) collective-permute-start(bf16[528,256]{1,0:T(8,128)(2,1)S(1)} %project.2.refs_8_), channel_id=1, source_target_pairs={{0,16},{1,17},{2,18},{3,19},{4,20},{5,21},{6,22},{7,23},{8,24},{9,... | collective-permute-start | bytes 811016 | tf_op jit(solution)/shard_map/ppermute | solution.py:31
  52.2 1.0 copy-start.2
  61.0 1.6 %collective-permute-start.16 = (bf16[528,256]{1,0:T(8,128)(2,1)S(1)}, bf16[528,256]{1,0:T(8,128)(2,1)S(1)}, u32[]{:S(2)}, u32[]{:S(2)}) collective-permute-start(bf16[528,256]{1,0:T(8,128)(2,1)S(1)} %collective-permute-done.8.rest_0_), channel_id=1, source_target_pairs={{0,8},{1,9},{2,10},{3,11},{4,12},{5,13},{6,14},{7,15},{8,0},{9,1},... | collective-permute-start | bytes 811016 | tf_op jit(solution)/shard_map/ppermute | solution.py:31
  64.4 10.2 %collective-permute-start.19 = (bf16[64,1152]{1,0:T(8,128)(2,1)S(1)}, bf16[64,1152]{1,0:T(8,128)(2,1)S(1)}, u32[]{:S(2)}, u32[]{:S(2)}) collective-permute-start(bf16[64,1152]{1,0:T(8,128)(2,1)S(1)} %attend_far.7), channel_id=1, source_target_pairs={{0,192},{1,193},{2,194},{3,195},{4,196},{5,197},{6,198},{7,199},{8... | collective-permute-start | bytes 442376 | tf_op jit(solution)/shard_map/ppermute | solution.py:31
  69.1 7.6 %collective-permute-start.18 = (bf16[64,1152]{1,0:T(8,128)(2,1)S(1)}, bf16[64,1152]{1,0:T(8,128)(2,1)S(1)}, u32[]{:S(2)}, u32[]{:S(2)}) collective-permute-start(bf16[64,1152]{1,0:T(8,128)(2,1)S(1)} %attend_far.6), channel_id=1, source_target_pairs={{0,128},{1,129},{2,130},{3,131},{4,132},{5,133},{6,134},{7,135},{8... | collective-permute-start | bytes 442376 | tf_op jit(solution)/shard_map/ppermute | solution.py:31
  71.2 23.6 %copy-start.1 = (bf16[4,1024,256]{2,1,0:T(8,128)(2,1)S(1)}, bf16[4,1024,256]{2,1,0:T(8,128)(2,1)}, u32[]{:S(2)}) copy-start(bf16[4,1024,256]{2,1,0:T(8,128)(2,1)} %all-gather.2.cloned.1.call-done.weights) | copy-start | bytes 6291460
  71.2 6.4 %collective-permute-start.17 = (bf16[64,1152]{1,0:T(8,128)(2,1)S(1)}, bf16[64,1152]{1,0:T(8,128)(2,1)S(1)}, u32[]{:S(2)}, u32[]{:S(2)}) collective-permute-start(bf16[64,1152]{1,0:T(8,128)(2,1)S(1)} %attend_far.5), channel_id=1, source_target_pairs={{0,64},{1,65},{2,66},{3,67},{4,68},{5,69},{6,70},{7,71},{8,72},{9,... | collective-permute-start | bytes 442376 | tf_op jit(solution)/shard_map/ppermute | solution.py:31
  74.6 48.8 %copy-start.9 = (bf16[128,256]{1,0:T(8,128)(2,1)S(1)}, bf16[128,256]{1,0:T(8,128)(2,1)}, u32[]{:S(2)}) copy-start(bf16[128,256]{1,0:T(8,128)(2,1)} %param.11) | copy-start | bytes 196612
  78.2 9.4 %collective-permute-start.20 = (bf16[64,1152]{1,0:T(8,128)(2,1)S(1)}, bf16[64,1152]{1,0:T(8,128)(2,1)S(1)}, u32[]{:S(2)}, u32[]{:S(2)}) collective-permute-start(bf16[64,1152]{1,0:T(8,128)(2,1)S(1)} %fold.2.refs_0_), channel_id=1, source_target_pairs={{0,32},{1,33},{2,34},{3,35},{4,36},{5,37},{6,38},{7,39},{8,40},{9,... | collective-permute-start | bytes 442376 | tf_op jit(solution)/shard_map/ppermute | solution.py:31
  87.9 5.5 %collective-permute-start.21 = (bf16[64,1024]{1,0:T(8,128)(2,1)S(1)}, bf16[64,1024]{1,0:T(8,128)(2,1)S(1)}, u32[]{:S(2)}, u32[]{:S(2)}) collective-permute-start(bf16[64,1024]{1,0:T(8,128)(2,1)S(1)} %fold.3.r0), channel_id=1, source_target_pairs={{0,16},{1,17},{2,18},{3,19},{4,20},{5,21},{6,22},{7,23},{8,24},{9,... | collective-permute-start | bytes 393224 | tf_op jit(solution)/shard_map/ppermute | solution.py:31
  88.0 5.4 %collective-permute-start.22 = (bf16[64,1024]{1,0:T(8,128)(2,1)S(1)}, bf16[64,1024]{1,0:T(8,128)(2,1)S(1)}, u32[]{:S(2)}, u32[]{:S(2)}) collective-permute-start(bf16[64,1024]{1,0:T(8,128)(2,1)S(1)} %fold.3.r0), channel_id=1, source_target_pairs={{0,8},{1,9},{2,10},{3,11},{4,12},{5,13},{6,14},{7,15},{8,0},{9,1},... | collective-permute-start | bytes 393224 | tf_op jit(solution)/shard_map/ppermute | solution.py:31
  93.5 1.3 %collective-permute-start.23 = (bf16[64,1024]{1,0:T(8,128)(2,1)S(1)}, bf16[64,1024]{1,0:T(8,128)(2,1)S(1)}, u32[]{:S(2)}, u32[]{:S(2)}) collective-permute-start(bf16[64,1024]{1,0:T(8,128)(2,1)S(1)} %collective-permute-done.21.r1), channel_id=1, source_target_pairs={{0,8},{1,9},{2,10},{3,11},{4,12},{5,13},{6,14},{7,15},{8,0},{9,1},... | collective-permute-start | bytes 393224 | tf_op jit(solution)/shard_map/ppermute | solution.py:31
  96.1 8.9 %collective-permute-start.24 = (bf16[256,256]{1,0:T(8,128)(2,1)S(1)}, bf16[256,256]{1,0:T(8,128)(2,1)S(1)}, u32[]{:S(2)}, u32[]{:S(2)}) collective-permute-start(bf16[256,256]{1,0:T(8,128)(2,1)S(1)} %get-tuple-element.35), channel_id=1, source_target_pairs={{0,0},{1,1},{2,2},{3,3},{4,4},{5,5},{6,6},{7,7},{8,8},{9,9},{10,10... | collective-permute-start | bytes 393224 | tf_op jit(solution)/shard_map/ppermute | solution.py:31
  99.7 7.3 %collective-permute-start.25 = (bf16[256,256]{1,0:T(8,128)(2,1)S(1)}, bf16[256,256]{1,0:T(8,128)(2,1)S(1)}, u32[]{:S(2)}, u32[]{:S(2)}) collective-permute-start(bf16[256,256]{1,0:T(8,128)(2,1)S(1)} %get-tuple-element.36), channel_id=1, source_target_pairs={{0,64},{1,65},{2,66},{3,67},{4,68},{5,69},{6,70},{7,71},{8,72},{9,... | collective-permute-start | bytes 393224 | tf_op jit(solution)/shard_map/ppermute | solution.py:31
  102.4 8.8 %collective-permute-start.26 = (bf16[256,256]{1,0:T(8,128)(2,1)S(1)}, bf16[256,256]{1,0:T(8,128)(2,1)S(1)}, u32[]{:S(2)}, u32[]{:S(2)}) collective-permute-start(bf16[256,256]{1,0:T(8,128)(2,1)S(1)} %get-tuple-element.37), channel_id=1, source_target_pairs={{0,128},{1,129},{2,130},{3,131},{4,132},{5,133},{6,134},{7,135},{8... | collective-permute-start | bytes 393224 | tf_op jit(solution)/shard_map/ppermute | solution.py:31
  102.5 12.0 %collective-permute-start.27 = (bf16[256,256]{1,0:T(8,128)(2,1)S(1)}, bf16[256,256]{1,0:T(8,128)(2,1)S(1)}, u32[]{:S(2)}, u32[]{:S(2)}) collective-permute-start(bf16[256,256]{1,0:T(8,128)(2,1)S(1)} %get-tuple-element.38), channel_id=1, source_target_pairs={{0,192},{1,193},{2,194},{3,195},{4,196},{5,197},{6,198},{7,199},{8... | collective-permute-start | bytes 393224 | tf_op jit(solution)/shard_map/ppermute | solution.py:31
  115.1 8.3 %collective-permute-start.28 = (bf16[128,256]{1,0:T(8,128)(2,1)S(1)}, bf16[128,256]{1,0:T(8,128)(2,1)S(1)}, u32[]{:S(2)}, u32[]{:S(2)}) collective-permute-start(bf16[128,256]{1,0:T(8,128)(2,1)S(1)} %get-tuple-element.40), channel_id=1, source_target_pairs={{0,1},{1,0},{2,3},{3,2},{4,5},{5,4},{6,7},{7,6},{8,9},{9,8},{10,11... | collective-permute-start | bytes 196616 | tf_op jit(solution)/shard_map/ppermute | solution.py:31
Sparse Core Ops, SparseCore 0:
  9.2 39.6 all-gather.1
